TPU v7x, 512 devices: a whole 4x8x8 slice. The times are simulated.
512 devices in a mesh: row: 32 (over x, z_hi, core), col: 16 (over y, z_lo).
Axes of the slice: x: 4, y: 8, z: 8 (z_hi: 4, z_lo: 2; z = z_hi * 2 + z_lo), core: 2. Of those that a mesh axis runs over, the one named last changes fastest.
Arguments:
- electric_x: float32 [192, 512, 128], P('col', 'row'), may hold values from -6 to 6
- electric_y: float32 [192, 512, 128], P('col', 'row'), may hold values from -6 to 6
- electric_z: float32 [192, 512, 128], P('col', 'row'), may hold values from -6 to 6
- magnetic_x: float32 [192, 512, 128], P('col', 'row'), may hold values from -6 to 6
- magnetic_y: float32 [192, 512, 128], P('col', 'row'), may hold values from -6 to 6
- magnetic_z: float32 [192, 512, 128], P('col', 'row'), may hold values from -6 to 6
- tissue: int32 [192, 512, 128], P('col', 'row'), may hold values from 0 to 63
- permittivity: float32 [64], replicated, may hold values from 1 to 60
- conductivity: float32 [64], replicated, may hold values from 0 to 1.5
Outputs:
- next_ex: float32 [192, 512, 128], P('col', 'row')
- next_ey: float32 [192, 512, 128], P('col', 'row')
- next_ez: float32 [192, 512, 128], P('col', 'row')
- next_hx: float32 [192, 512, 128], P('col', 'row')
- next_hy: float32 [192, 512, 128], P('col', 'row')
- next_hz: float32 [192, 512, 128], P('col', 'row')
All inputs are finite; a program needn't handle non-finite values.
Results may differ from a plain program's by a relative error of at most 0.0003.
Values sent between devices are 32-bit elements; how exact they have to be, the bound alone decides.
A program may use at most 64 MiB of HBM per device.

v0:
```python
import functools

import jax
import jax.numpy as jnp
from jax import lax
from jax.experimental import pallas as pl
from jax.experimental.pallas import tpu as pltpu
from jax.sharding import PartitionSpec as P

MESH = pl.DeviceIdType.MESH
half_step = 32.0
inv_half = 1.0 / half_step
TILE = 8


def roll(values, shift, axis):
    return pltpu.roll(values, shift, axis)


def cyclic_setup(low, up, diag, axis, keep):
    n = diag.shape[axis]
    stride = 1
    level = 0
    while stride < n:
        inv = 1.0 / diag
        from_low = low * roll(inv, stride, axis)
        from_up = up * roll(inv, n - stride, axis)
        diag = diag - from_low * low - from_up * up
        if 2 * stride < n:
            low = from_low * roll(low, stride, axis)
            up = from_up * roll(up, n - stride, axis)
        keep(2 * level, from_low)
        keep(2 * level + 1, from_up)
        stride, level = 2 * stride, level + 1
    keep(2 * level, 1.0 / diag)


def cyclic_solve(rhs, axis, kept):
    n = rhs.shape[axis]
    stride = 1
    level = 0
    while stride < n:
        rhs = (
            rhs
            + kept(2 * level) * roll(rhs, stride, axis)
            + kept(2 * level + 1) * roll(rhs, n - stride, axis)
        )
        stride, level = 2 * stride, level + 1
    return rhs * kept(2 * level)


def levels_of(n):
    return (n - 1).bit_length()


def kernel(sizes, *refs):
    lz, ly, nx, nrow, ncol, nt = sizes
    cells = lz * ly
    (ex_h, ey_h, ez_h, mx_h, my_h, mz_h, tis_h, eps_s, sig_s) = refs[:9]
    (nex, ney, nez, nhx, nhy, nhz) = refs[9:15]
    (
        ex, ey, ez, mx, my, mz, tis,
        recip, keepf, ax, ay, az,
        fx, fy, fz, ex1, ey1, ez1, dex, dey, dez, cx, cy, cz,
        sh0, sh1, sh2, sh3,
        xfac,
        uy, ry, vy, uz, rz, vz,
        send_y, send_z, gat_y, gat_z, ret_y, ret_z, res_y, res_z,
        fac_y, fac_z, mid_y, mid_z,
        halo_mx_s, halo_ez_s, halo_mx, halo_ez, halo_my, halo_ex,
        load_sem, halo_send, halo_recv, sems,
    ) = refs[15:]

    me_r, me_c = lax.axis_index("row"), lax.axis_index("col")
    gate_r = jnp.where(me_r > 0, 1.0, 0.0)
    gate_c = jnp.where(me_c > 0, 1.0, 0.0)
    gate_r_end = jnp.where(me_r < nrow - 1, 1.0, 0.0)
    gate_c_end = jnp.where(me_c < ncol - 1, 1.0, 0.0)

    def at_row(p):
        return (p, me_c)

    def at_col(p):
        return (me_r, p)

    loads = [
        pltpu.make_async_copy(src, dst, load_sem.at[i])
        for i, (src, dst) in enumerate(
            ((tis_h, tis), (mx_h, mx), (ez_h, ez), (my_h, my), (ex_h, ex), (ey_h, ey), (mz_h, mz))
        )
    ]
    for load in loads:
        load.start()

    barrier = pltpu.get_barrier_semaphore()

    def greet_row(i, _):
        pl.semaphore_signal(
            barrier, inc=1, device_id=at_row(lax.rem(me_r + 1 + i, nrow)), device_id_type=MESH
        )
        return 0

    def greet_col(i, _):
        pl.semaphore_signal(
            barrier, inc=1, device_id=at_col(lax.rem(me_c + 1 + i, ncol)), device_id_type=MESH
        )
        return 0

    lax.fori_loop(0, nrow - 1, greet_row, 0)
    lax.fori_loop(0, ncol - 1, greet_col, 0)

    loads[0].wait()
    part = cells // 2
    group = 4

    def look_up(c, _):
        at = pl.ds(pl.multiple_of(c * part, 8), part)
        label = tis[at, :]

        def tissues(g, carry):
            eps, sig = carry
            for j in range(group):
                t = g * group + j
                same = label == t
                eps = jnp.where(same, eps_s[t], eps)
                sig = jnp.where(same, sig_s[t], sig)
            return eps, sig

        zero = jnp.zeros(label.shape, jnp.float32)
        eps, sig = lax.fori_loop(0, nt // group, tissues, (zero, zero))
        loss = sig * (0.5 * half_step)
        scale = inv_half * inv_half
        recip[at, :] = (eps + loss) * scale
        keepf[at, :] = (eps - loss) * scale
        return 0

    lax.fori_loop(0, 2, look_up, 0)

    for load in loads[1:]:
        load.wait()

    def row_y(ref, i):
        return ref[pl.ds(i, lz, stride=ly), :]

    def put_y(ref, i, values):
        ref[pl.ds(i, lz, stride=ly), :] = values

    def row_z(ref, i):
        return ref[pl.ds(i * ly, ly), :]

    def put_z(ref, i, values):
        ref[pl.ds(i * ly, ly), :] = values

    halo_mx_s[pl.ds(0, lz), :] = row_y(mx, ly - 1)
    halo_ez_s[pl.ds(0, lz), :] = row_y(ez, 0)
    pl.semaphore_wait(barrier, nrow + ncol - 2)

    up_r, down_r = lax.rem(me_r + 1, nrow), lax.rem(me_r + nrow - 1, nrow)
    up_c, down_c = lax.rem(me_c + 1, ncol), lax.rem(me_c + ncol - 1, ncol)

    def remote(src, dst, send_sem, recv_sem, device):
        return pltpu.make_async_remote_copy(
            src_ref=src,
            dst_ref=dst,
            send_sem=send_sem,
            recv_sem=recv_sem,
            device_id=device,
            device_id_type=MESH,
        )

    halos = [
        remote(halo_mx_s, halo_mx, halo_send.at[0], halo_recv.at[0], at_row(up_r)),
        remote(halo_ez_s, halo_ez, halo_send.at[1], halo_recv.at[1], at_row(down_r)),
        remote(my.at[pl.ds(cells - ly, ly), :], halo_my, halo_send.at[2], halo_recv.at[2], at_col(up_c)),
        remote(ex.at[pl.ds(0, ly), :], halo_ex, halo_send.at[3], halo_recv.at[3], at_col(down_c)),
    ]
    for halo in halos:
        halo.start()

    def matrix_forward(n, row, first_gate, u_ref, r_ref, send, count):
        diag = row(recip, 0) + (2.0 - first_gate)
        inv = 1.0 / diag
        reach = inv
        beta = reach
        u_ref[0], r_ref[0] = reach, inv
        for i in range(1, n - 1):
            diag = row(recip, i) + 2.0 - inv
            inv = 1.0 / diag
            further = reach * inv
            beta = beta + reach * further
            reach = further
            u_ref[i], r_ref[i] = reach, inv
        send[pl.ds(0, count, stride=TILE), :] = row(recip, n - 1) + 2.0 - inv
        send[pl.ds(1, count, stride=TILE), :] = beta
        send[pl.ds(2, count, stride=TILE), :] = reach

    def rhs_forward(n, row, f_ref, u_ref, r_ref, v_ref, send, count, passed_on):
        value = row(f_ref, 0) * r_ref[0]
        psi = value
        v_ref[0] = value
        for i in range(1, n - 1):
            value = (row(f_ref, i) + value) * r_ref[i]
            psi = psi + u_ref[i - 1] * value
            v_ref[i] = value
        send[pl.ds(3, count, stride=TILE), :] = row(f_ref, n - 1) + value
        send[pl.ds(4, count, stride=TILE), :] = psi
        send[pl.ds(5, count, stride=TILE), :] = passed_on

    def back(n, row_put, u_ref, r_ref, v_ref, got, count, out, diff):
        before = got[pl.ds(0, count, stride=TILE), :] + got[pl.ds(3, count, stride=TILE), :]
        value = got[pl.ds(1, count, stride=TILE), :]
        row_put(out, n - 1, value)
        row_put(diff, n - 1, got[pl.ds(2, count, stride=TILE), :] - value)
        for i in range(n - 2, -1, -1):
            lower = (v_ref[i] + u_ref[i] * before) + r_ref[i] * value
            row_put(out, i, lower)
            row_put(diff, i, value - lower)
            value = lower

    first_r, first_c = 1.0 - gate_r, 1.0 - gate_c
    matrix_forward(ly, row_y, first_r, uy, ry, send_y, lz)
    matrix_forward(lz, row_z, first_c, uz, rz, send_z, ly)

    chunk = 32 if cells % 32 == 0 else 8

    def x_setup(c, _):
        at = pl.multiple_of(c * chunk, 8)
        diag = recip[pl.ds(at, chunk), :]
        lane = lax.broadcasted_iota(jnp.int32, diag.shape, 1)
        low = jnp.where(lane == 0, 0.0, 1.0)
        up = jnp.where(lane == nx - 1, 0.0, 1.0)

        def keep(slot, values):
            xfac[slot, pl.ds(at, chunk), :] = values

        cyclic_setup(low, up, diag + 1.0 + low, 1, keep)
        return 0

    lax.fori_loop(0, cells // chunk, x_setup, 0)

    lane = lax.broadcasted_iota(jnp.int32, (cells, nx), 1)

    def before_x(values):
        return jnp.where(lane == 0, 0.0, roll(values, 1, 1))

    def after_x(values):
        return jnp.where(lane == nx - 1, 0.0, roll(values, nx - 1, 1))

    def before_y(values, first, shifted):
        shifted[...] = roll(values, 1, 0)
        put_y(shifted, 0, first)
        return shifted[...]

    def after_y(values, last, shifted):
        shifted[...] = roll(values, cells - 1, 0)
        put_y(shifted, ly - 1, last)
        return shifted[...]

    def before_z(values, first):
        return jnp.concatenate([first, values[: cells - ly]], axis=0)

    def after_z(values, last):
        return jnp.concatenate([values[ly:], last], axis=0)

    def x_solve(f_ref, write):
        def lines(c, _):
            at = pl.multiple_of(c * chunk, 8)
            solved = cyclic_solve(
                f_ref[pl.ds(at, chunk), :], 1, lambda slot: xfac[slot, pl.ds(at, chunk), :]
            )
            column = lax.broadcasted_iota(jnp.int32, solved.shape, 1)
            ahead = jnp.where(column == nx - 1, 0.0, roll(solved, nx - 1, 1)) - solved
            write(pl.ds(at, chunk), solved, ahead)
            return 0

        lax.fori_loop(0, cells // chunk, lines, 0)

    zero_y = jnp.zeros((lz, nx), jnp.float32)
    zero_z = jnp.zeros((ly, nx), jnp.float32)

    mz_v = mz[...]
    ey_v = ey[...]
    ay_v = mz_v * inv_half - (after_x(ey_v) - ey_v)
    ay[...] = ay_v
    for halo in halos:
        halo.wait_recv()
    my_v = my[...]
    my_before = before_z(my_v, halo_my[...] * gate_c)
    fx[...] = (
        keepf[...] * ex[...] - (my_v - my_before) * inv_half + (ay_v - before_y(ay_v, zero_y, sh0))
    )
    ez_v = ez[...]
    mx_v = mx[...]
    ez_after = after_y(ez_v, halo_ez[pl.ds(0, lz), :] * gate_r_end, sh1)
    az_v = mx_v * inv_half - (ez_after - ez_v)
    az[...] = az_v
    fy[...] = (
        keepf[...] * ey_v - (mz_v - before_x(mz_v)) * inv_half + (az_v - before_z(az_v, zero_z))
    )

    me_owner_j = lax.div(lz * me_r + nrow - 1, nrow)

    def owner_of(j):
        return lax.div(j * nrow, lz)

    owns = jnp.logical_and(me_owner_j < lz, owner_of(me_owner_j) == me_r)
    others = jnp.logical_not(owns)

    def tile(ref, i):
        return ref.at[pl.ds(pl.multiple_of(i * TILE, TILE), TILE), :]

    def wait_send(ref, count, sem):
        part_of = ref.at[pl.ds(0, count * TILE), :]
        remote(part_of, part_of, sem, sem, at_row(up_r)).wait_send()

    def wait_recv(ref, count, sem):
        part_of = ref.at[pl.ds(0, count * TILE), :]
        remote(part_of, part_of, sem, sem, at_row(up_r)).wait_recv()

    def scatter_y(step):
        def to_owner(i, _):
            j = lax.rem(me_r + i, lz)
            owner = owner_of(j)

            @pl.when(owner != me_r)
            def _():
                remote(
                    tile(send_y, j), tile(gat_y.at[step], me_r), sems.at[0, step], sems.at[1, step], at_row(owner)
                ).start()

            return 0

        lax.fori_loop(0, lz, to_owner, 0)

        @pl.when(owns)
        def _():
            gat_y[step, pl.ds(pl.multiple_of(me_r * TILE, TILE), TILE), :] = send_y[
                pl.ds(pl.multiple_of(me_owner_j * TILE, TILE), TILE), :
            ]

    def scatter_z(step):
        def to_owner(i, _):
            q = lax.rem(me_c + 1 + i, ncol)
            remote(
                tile(send_z, q), tile(gat_z.at[step], me_c), sems.at[2, step], sems.at[3, step], at_col(q)
            ).start()
            return 0

        lax.fori_loop(0, ncol - 1, to_owner, 0)
        own = pl.ds(pl.multiple_of(me_c * TILE, TILE), TILE)
        gat_z[step, own, :] = send_z[own, :]

    def solve_owned(step, n, got, fac, mid, ret):
        def read(r):
            return got[step, pl.ds(r, n, stride=TILE), :]

        place = lax.broadcasted_iota(jnp.int32, (n, nx), 0)
        starts, ends = place == 0, place == n - 1
        if step == 0:
            beta = read(1)
            link = jnp.where(starts, 0.0, read(2))
            beta_up = jnp.where(ends, 0.0, roll(beta, n - 1, 0))
            link_up = jnp.where(ends, 0.0, roll(link, n - 1, 0))
            mid[0], mid[1], mid[2], mid[3] = beta, link, beta_up, link_up

            def keep(slot, values):
                fac[slot] = values

            cyclic_setup(link, link_up, read(0) - beta_up, 0, keep)
        else:
            beta, link, beta_up, link_up = mid[0], mid[1], mid[2], mid[3]
        added = jnp.where(starts, 0.0, roll(read(5), 1, 0))
        phi = read(3) + link * added
        psi = read(4) + beta * added
        psi_up = jnp.where(ends, 0.0, roll(psi, n - 1, 0))
        last = cyclic_solve(phi + psi_up, 0, lambda slot: fac[slot])
        before = jnp.where(starts, 0.0, roll(last, 1, 0))
        after = psi_up + beta_up * last + link_up * roll(last, n - 1, 0)
        ret[step, pl.ds(0, n, stride=TILE), :] = before
        ret[step, pl.ds(1, n, stride=TILE), :] = last
        ret[step, pl.ds(2, n, stride=TILE), :] = after
        ret[step, pl.ds(3, n, stride=TILE), :] = added

    def own_y(step):
        @pl.when(owns)
        def _():
            wait_recv(gat_y.at[step], nrow - 1, sems.at[1, step])
            solve_owned(step, nrow, gat_y, fac_y, mid_y, ret_y)

            def give(i, _):
                q = lax.rem(me_r + 1 + i, nrow)
                remote(
                    tile(ret_y.at[step], q), tile(res_y.at[step], me_owner_j), sems.at[4, step], sems.at[5, step], at_row(q)
                ).start()
                return 0

            lax.fori_loop(0, nrow - 1, give, 0)
            res_y[step, pl.ds(pl.multiple_of(me_owner_j * TILE, TILE), TILE), :] = ret_y[
                step, pl.ds(pl.multiple_of(me_r * TILE, TILE), TILE), :
            ]

    def own_z(step):
        wait_recv(gat_z.at[step], ncol - 1, sems.at[3, step])
        solve_owned(step, ncol, gat_z, fac_z, mid_z, ret_z)

        def give(i, _):
            q = lax.rem(me_c + 1 + i, ncol)
            remote(
                tile(ret_z.at[step], q), tile(res_z.at[step], me_c), sems.at[6, step], sems.at[7, step], at_col(q)
            ).start()
            return 0

        lax.fori_loop(0, ncol - 1, give, 0)
        own = pl.ds(pl.multiple_of(me_c * TILE, TILE), TILE)
        res_z[step, own, :] = ret_z[step, own, :]

    def wait_sent(step):
        @pl.when(owns)
        def _():
            wait_send(send_y, lz - 1, sems.at[0, step])
            wait_send(ret_y.at[step], nrow - 1, sems.at[4, step])

        @pl.when(others)
        def _():
            wait_send(send_y, lz, sems.at[0, step])

        wait_send(send_z, ncol - 1, sems.at[2, step])
        wait_send(ret_z.at[step], ncol - 1, sems.at[6, step])

    def wait_y(step):
        @pl.when(owns)
        def _():
            wait_recv(res_y.at[step], lz - 1, sems.at[5, step])

        @pl.when(others)
        def _():
            wait_recv(res_y.at[step], lz, sems.at[5, step])

    def wait_z(step):
        wait_recv(res_z.at[step], ncol - 1, sems.at[7, step])

    rhs_forward(ly, row_y, fx, uy, ry, vy, send_y, lz, -row_y(ay, ly - 1))
    scatter_y(0)
    rhs_forward(lz, row_z, fy, uz, rz, vz, send_z, ly, -row_z(az, lz - 1))
    scatter_z(0)

    ex_v = ex[...]
    ax_v = my[...] * inv_half - (after_z(ex_v, halo_ex[...] * gate_c_end) - ex_v)
    ax[...] = ax_v
    mx_v = mx[...]
    mx_before = before_y(mx_v, halo_mx[pl.ds(0, lz), :] * gate_r, sh2)
    fz[...] = (
        keepf[...] * ez[...] - (mx_v - mx_before) * inv_half + (ax_v - before_x(ax_v))
    )

    def keep_half(at, solved, ahead):
        ez1[at, :] = solved
        dez[at, :] = ahead

    x_solve(fz, keep_half)
    cz_v = ax[...] + 2.0 * dez[...]
    cz[...] = cz_v
    hy_v = ax[...] + dez[...]
    fz[...] = keepf[...] * ez1[...] + (hy_v - before_x(hy_v))
    fx[...] = before_z(cz_v, zero_z) - cz_v

    own_z(0)
    own_y(0)
    wait_sent(0)

    wait_z(0)
    back(lz, put_z, uz, rz, vz, res_z.at[0], ly, ey1, dey)
    wait_y(0)
    back(ly, put_y, uy, ry, vy, res_y.at[0], lz, ex1, dex)

    dex_v, dey_v = dex[...], dey[...]
    ay_v, az_v = ay[...], az[...]
    cx_v, cy_v = ay_v + 2.0 * dex_v, az_v + 2.0 * dey_v
    cx[...], cy[...] = cx_v, cy_v
    hz_v = ay_v + dex_v
    hz_first = (
        row_y(ex1, 0) - res_y[0, pl.ds(0, lz, stride=TILE), :] - res_y[0, pl.ds(3, lz, stride=TILE), :]
    ) * gate_r
    fx[...] = fx[...] + keepf[...] * ex1[...] + (hz_v - before_y(hz_v, hz_first, sh0))
    fz[...] = fz[...] - (cy_v - before_y(cy_v, zero_y, sh1))

    rhs_forward(ly, row_y, fz, uy, ry, vy, send_y, lz, row_y(cy, ly - 1))
    scatter_y(1)
    rhs_forward(lz, row_z, fx, uz, rz, vz, send_z, ly, row_z(cz, lz - 1))
    scatter_z(1)

    hx_v = az[...] + dey[...]
    hx_first = (
        row_z(ey1, 0) - res_z[0, pl.ds(0, ly, stride=TILE), :] - res_z[0, pl.ds(3, ly, stride=TILE), :]
    ) * gate_c
    cx_v = cx[...]
    fy[...] = keepf[...] * ey1[...] + (hx_v - before_z(hx_v, hx_first)) - (cx_v - before_x(cx_v))

    def write_y(at, solved, ahead):
        ney[at, :] = solved
        nhz[at, :] = (cx[at, :] - ahead) * half_step

    x_solve(fy, write_y)

    own_z(1)
    own_y(1)
    wait_z(1)
    back(lz, put_z, uz, rz, vz, res_z.at[1], ly, nex, dez)
    nhy[...] = (cz[...] - dez[...]) * half_step
    wait_y(1)
    back(ly, put_y, uy, ry, vy, res_y.at[1], lz, nez, dex)
    nhx[...] = (cy[...] - dex[...]) * half_step
    wait_sent(1)
    for halo in halos:
        halo.wait_send()


def solution(mesh):
    nrow, ncol = mesh.shape["row"], mesh.shape["col"]

    def per_device(ex, ey, ez, mx, my, mz, tissue, permittivity, conductivity):
        lz, ly, nx = ex.shape
        cells, nt = lz * ly, permittivity.shape[0]
        f32 = jnp.float32
        flat = [a.reshape(cells, nx) for a in (ex, ey, ez, mx, my, mz, tissue)]
        whole = pltpu.VMEM((cells, nx), f32)
        pad_z = -(-lz // 8) * 8
        slots = lambda n: 2 * levels_of(n) + 1
        scratch = (
            [whole] * 6
            + [pltpu.VMEM((cells, nx), jnp.int32)]
            + [whole] * 21
            + [pltpu.VMEM((slots(nx), cells, nx), f32)]
            + [pltpu.VMEM((ly - 1, lz, nx), f32)] * 3
            + [pltpu.VMEM((lz - 1, ly, nx), f32)] * 3
            + [pltpu.VMEM((lz * TILE, nx), f32), pltpu.VMEM((ly * TILE, nx), f32)]
            + [pltpu.VMEM((2, nrow * TILE, nx), f32), pltpu.VMEM((2, ncol * TILE, nx), f32)] * 2
            + [pltpu.VMEM((2, lz * TILE, nx), f32), pltpu.VMEM((2, ly * TILE, nx), f32)]
            + [pltpu.VMEM((slots(nrow), nrow, nx), f32), pltpu.VMEM((slots(ncol), ncol, nx), f32)]
            + [pltpu.VMEM((4, nrow, nx), f32), pltpu.VMEM((4, ncol, nx), f32)]
            + [pltpu.VMEM((pad_z, nx), f32)] * 4
            + [pltpu.VMEM((ly, nx), f32)] * 2
            + [
                pltpu.SemaphoreType.DMA((7,)),
                pltpu.SemaphoreType.DMA((4,)),
                pltpu.SemaphoreType.DMA((4,)),
                pltpu.SemaphoreType.DMA((8, 2)),
            ]
        )
        outs = pl.pallas_call(
            functools.partial(kernel, (lz, ly, nx, nrow, ncol, nt)),
            out_shape=[jax.ShapeDtypeStruct((cells, nx), f32)] * 6,
            in_specs=[pl.BlockSpec(memory_space=pl.ANY)] * 7 + [pl.BlockSpec(memory_space=pltpu.SMEM)] * 2,
            out_specs=[pl.BlockSpec(memory_space=pltpu.VMEM)] * 6,
            scratch_shapes=scratch,
            compiler_params=pltpu.CompilerParams(
                collective_id=0, has_side_effects=True, vmem_limit_bytes=32 * 1024 * 1024
            ),
        )(*flat, permittivity, conductivity)
        return tuple(o.reshape(lz, ly, nx) for o in outs)

    cut = P("col", "row", None)
    return jax.shard_map(
        per_device,
        mesh=mesh,
        in_specs=(cut,) * 7 + (P(), P()),
        out_specs=(cut,) * 6,
        check_vma=False,
    )
```

profile of v0, /device:TPU:1, one launch (start us, length us, event | category | flops | bytes accessed | tf_op | source)
XLA Modules:
  0.0 58.7 jit_solution(2865472246841188508)
XLA Ops:
  0.6 0.0 copy-start.7
  0.6 0.0 copy-start.8
  0.7 0.6 %copy-done.7 = f32[64]{0:T(128)S(1)} copy-done((f32[64]{0:T(128)S(1)}, f32[64]{0:T(128)}, u32[]{:S(2)}) %copy-start.7) | copy-done | bytes 280
  1.3 0.0 copy-done.8
  1.3 0.0 copy-start
  1.3 0.9 %copy-done = f32[12,16,128]{2,1,0:T(8,128)S(1)} copy-done((f32[12,16,128]{2,1,0:T(8,128)S(1)}, f32[12,16,128]{2,1,0:T(8,128)}, u32[]{:S(2)}) %copy-start) | copy-done | bytes 98328
  2.2 0.0 copy-start.1
  2.2 0.9 %copy-done.1 = f32[12,16,128]{2,1,0:T(8,128)S(1)} copy-done((f32[12,16,128]{2,1,0:T(8,128)S(1)}, f32[12,16,128]{2,1,0:T(8,128)}, u32[]{:S(2)}) %copy-start.1) | copy-done | bytes 98328
  3.1 0.0 copy-start.2
  3.1 0.9 %copy-done.2 = f32[12,16,128]{2,1,0:T(8,128)S(1)} copy-done((f32[12,16,128]{2,1,0:T(8,128)S(1)}, f32[12,16,128]{2,1,0:T(8,128)}, u32[]{:S(2)}) %copy-start.2) | copy-done | bytes 98328
  4.0 0.0 copy-start.3
  4.0 0.9 %copy-done.3 = f32[12,16,128]{2,1,0:T(8,128)S(1)} copy-done((f32[12,16,128]{2,1,0:T(8,128)S(1)}, f32[12,16,128]{2,1,0:T(8,128)}, u32[]{:S(2)}) %copy-start.3) | copy-done | bytes 98328
  4.9 0.0 copy-start.4
  4.9 0.9 %copy-done.4 = f32[12,16,128]{2,1,0:T(8,128)S(1)} copy-done((f32[12,16,128]{2,1,0:T(8,128)S(1)}, f32[12,16,128]{2,1,0:T(8,128)}, u32[]{:S(2)}) %copy-start.4) | copy-done | bytes 98328
  5.8 0.0 copy-start.5
  5.8 0.9 %copy-done.5 = f32[12,16,128]{2,1,0:T(8,128)S(1)} copy-done((f32[12,16,128]{2,1,0:T(8,128)S(1)}, f32[12,16,128]{2,1,0:T(8,128)}, u32[]{:S(2)}) %copy-start.5) | copy-done | bytes 98328
  6.7 0.0 copy-start.6
  6.7 0.9 %copy-done.6 = s32[12,16,128]{2,1,0:T(8,128)S(1)} copy-done((s32[12,16,128]{2,1,0:T(8,128)S(1)}, s32[12,16,128]{2,1,0:T(8,128)}, u32[]{:S(2)}) %copy-start.6) | copy-done | bytes 98328
  7.6 47.3 %shard_map.136 = (f32[192,128]{1,0:T(8,128)S(1)}, f32[192,128]{1,0:T(8,128)S(1)}, f32[192,128]{1,0:T(8,128)S(1)}, f32[192,128]{1,0:T(8,128)S(1)}, f32[192,128]{1,0:T(8,128)S(1)}, /*index=5*/f32[192,128]{1,0:T(8,128)S(1)}) custom-call(f32[192,128]{1,0:T(8,128)S(1)} %bitcast.19, f32[192,128]{1,0:T(8,128)S(1)} %bitcast.20, f32[192,128]{1,0:T(8,128)S(1)} %bitcast.21, ...), custom_call_target="tpu_custom_call" | custom-call | tf_op jit(solution)/shard_map/pallas_call | solution.py:550
  54.8 0.6 %copy.21 = f32[12,16,128]{2,1,0:T(8,128)} copy(f32[12,16,128]{2,1,0:T(8,128)S(1)} %bitcast.18) | data formatting | bytes 196608
  55.5 0.6 %copy.22 = f32[12,16,128]{2,1,0:T(8,128)} copy(f32[12,16,128]{2,1,0:T(8,128)S(1)} %bitcast.17) | data formatting | bytes 196608
  56.1 0.6 %copy.23 = f32[12,16,128]{2,1,0:T(8,128)} copy(f32[12,16,128]{2,1,0:T(8,128)S(1)} %bitcast.16) | data formatting | bytes 196608
  56.8 0.6 %copy.24 = f32[12,16,128]{2,1,0:T(8,128)} copy(f32[12,16,128]{2,1,0:T(8,128)S(1)} %bitcast.15) | data formatting | bytes 196608
  57.4 0.6 %copy.25 = f32[12,16,128]{2,1,0:T(8,128)} copy(f32[12,16,128]{2,1,0:T(8,128)S(1)} %bitcast.14) | data formatting | bytes 196608
  58.0 0.6 %copy.26 = f32[12,16,128]{2,1,0:T(8,128)} copy(f32[12,16,128]{2,1,0:T(8,128)S(1)} %bitcast.13) | data formatting | bytes 196608
Async XLA Ops:
  0.6 0.7 %copy-start.7 = (f32[64]{0:T(128)S(1)}, f32[64]{0:T(128)}, u32[]{:S(2)}) copy-start(f32[64]{0:T(128)} %refs_7_.1) | copy-start | bytes 772
  0.6 0.7 %copy-start.8 = (f32[64]{0:T(128)S(1)}, f32[64]{0:T(128)}, u32[]{:S(2)}) copy-start(f32[64]{0:T(128)} %refs_8_.1) | copy-start | bytes 772
  1.3 0.9 %copy-start = (f32[12,16,128]{2,1,0:T(8,128)S(1)}, f32[12,16,128]{2,1,0:T(8,128)}, u32[]{:S(2)}) copy-start(f32[12,16,128]{2,1,0:T(8,128)} %param.9) | copy-start | bytes 294916
  2.2 0.9 %copy-start.1 = (f32[12,16,128]{2,1,0:T(8,128)S(1)}, f32[12,16,128]{2,1,0:T(8,128)}, u32[]{:S(2)}) copy-start(f32[12,16,128]{2,1,0:T(8,128)} %param.10) | copy-start | bytes 294916
  3.1 0.9 %copy-start.2 = (f32[12,16,128]{2,1,0:T(8,128)S(1)}, f32[12,16,128]{2,1,0:T(8,128)}, u32[]{:S(2)}) copy-start(f32[12,16,128]{2,1,0:T(8,128)} %param.11) | copy-start | bytes 294916
  4.0 0.9 %copy-start.3 = (f32[12,16,128]{2,1,0:T(8,128)S(1)}, f32[12,16,128]{2,1,0:T(8,128)}, u32[]{:S(2)}) copy-start(f32[12,16,128]{2,1,0:T(8,128)} %param.12) | copy-start | bytes 294916
  4.9 0.9 %copy-start.4 = (f32[12,16,128]{2,1,0:T(8,128)S(1)}, f32[12,16,128]{2,1,0:T(8,128)}, u32[]{:S(2)}) copy-start(f32[12,16,128]{2,1,0:T(8,128)} %param.13) | copy-start | bytes 294916
  5.8 0.9 %copy-start.5 = (f32[12,16,128]{2,1,0:T(8,128)S(1)}, f32[12,16,128]{2,1,0:T(8,128)}, u32[]{:S(2)}) copy-start(f32[12,16,128]{2,1,0:T(8,128)} %param.14) | copy-start | bytes 294916
  6.7 0.9 %copy-start.6 = (s32[12,16,128]{2,1,0:T(8,128)S(1)}, s32[12,16,128]{2,1,0:T(8,128)}, u32[]{:S(2)}) copy-start(s32[12,16,128]{2,1,0:T(8,128)} %param.15) | copy-start | bytes 294916
where the time goes:
time: 59 us; the launch traced here: 58.7 us
  Pallas kernels  47.3 us (80%)
  local copies, waits for them, and re-layouts  10.7 us (18%)
  between operations  0.67 us (1%)
    pallas_call x1, Pallas kernels, per_device(): pl.pallas_call(functools.partial(kernel, (lz, ly, nx, nrow, ncol, nt)), o...  47.3 us
    unnamed x24, local copies, waits for them, and re-layouts  10.7 us

commit v1 on v0

--- a/solution.py
+++ b/solution.py
@@ -11,28 +11,33 @@
 half_step = 32.0
 inv_half = 1.0 / half_step
 TILE = 8
+VMEM_BYTES = 56 * 1024 * 1024
 
 
 def roll(values, shift, axis):
     return pltpu.roll(values, shift, axis)
 
 
-def cyclic_setup(low, up, diag, axis, keep):
-    n = diag.shape[axis]
+def cyclic_setup(low, up, excess, axis, keep):
+    n = excess.shape[axis]
     stride = 1
     level = 0
     while stride < n:
-        inv = 1.0 / diag
+        inv = 1.0 / (low + up + excess)
         from_low = low * roll(inv, stride, axis)
         from_up = up * roll(inv, n - stride, axis)
-        diag = diag - from_low * low - from_up * up
+        excess = (
+            excess
+            + from_low * roll(excess, stride, axis)
+            + from_up * roll(excess, n - stride, axis)
+        )
         if 2 * stride < n:
             low = from_low * roll(low, stride, axis)
             up = from_up * roll(up, n - stride, axis)
         keep(2 * level, from_low)
         keep(2 * level + 1, from_up)
         stride, level = 2 * stride, level + 1
-    keep(2 * level, 1.0 / diag)
+    keep(2 * level, 1.0 / excess)
 
 
 def cyclic_solve(rhs, axis, kept):
@@ -56,19 +61,21 @@
 def kernel(sizes, *refs):
     lz, ly, nx, nrow, ncol, nt = sizes
     cells = lz * ly
-    (ex_h, ey_h, ez_h, mx_h, my_h, mz_h, tis_h, eps_s, sig_s) = refs[:9]
-    (nex, ney, nez, nhx, nhy, nhz) = refs[9:15]
+    (ex_h, ey_h, ez_h, mx_h, my_h, mz_h, tis_h, eps_h, sig_h) = refs[:9]
+    outs_h = refs[9:15]
     (
+        eps_s, sig_s,
         ex, ey, ez, mx, my, mz, tis,
-        recip, keepf, ax, ay, az,
+        nex, ney, nez, nhx, nhy, nhz,
+        recip, keepf, twice, gx, gy, gz, ax, ay, az,
         fx, fy, fz, ex1, ey1, ez1, dex, dey, dez, cx, cy, cz,
         sh0, sh1, sh2, sh3,
         xfac,
         uy, ry, vy, uz, rz, vz,
-        send_y, send_z, gat_y, gat_z, ret_y, ret_z, res_y, res_z,
+        send_y0, send_y1, send_z0, send_z1, gat_y, gat_z, ret_y, ret_z, res_y, res_z,
         fac_y, fac_z, mid_y, mid_z,
         halo_mx_s, halo_ez_s, halo_mx, halo_ez, halo_my, halo_ex,
-        load_sem, halo_send, halo_recv, sems,
+        load_sem, store_sem, halo_send, halo_recv, sems,
     ) = refs[15:]
 
     me_r, me_c = lax.axis_index("row"), lax.axis_index("col")
@@ -86,11 +93,30 @@
     loads = [
         pltpu.make_async_copy(src, dst, load_sem.at[i])
         for i, (src, dst) in enumerate(
-            ((tis_h, tis), (mx_h, mx), (ez_h, ez), (my_h, my), (ex_h, ex), (ey_h, ey), (mz_h, mz))
+            (
+                (eps_h, eps_s),
+                (sig_h, sig_s),
+                (tis_h, tis),
+                (mx_h, mx),
+                (ez_h, ez),
+                (my_h, my),
+                (ex_h, ex),
+                (ey_h, ey),
+                (mz_h, mz),
+            )
         )
     ]
     for load in loads:
         load.start()
+
+    stores = [
+        pltpu.make_async_copy(src, dst, store_sem.at[i])
+        for i, (src, dst) in enumerate(zip((nex, ney, nez, nhx, nhy, nhz), outs_h))
+    ]
+
+    def store(*which):
+        for i in which:
+            stores[i].start()
 
     barrier = pltpu.get_barrier_semaphore()
 
@@ -109,7 +135,8 @@
     lax.fori_loop(0, nrow - 1, greet_row, 0)
     lax.fori_loop(0, ncol - 1, greet_col, 0)
 
-    loads[0].wait()
+    for load in loads[:3]:
+        load.wait()
     part = cells // 2
     group = 4
 
@@ -132,11 +159,12 @@
         scale = inv_half * inv_half
         recip[at, :] = (eps + loss) * scale
         keepf[at, :] = (eps - loss) * scale
+        twice[at, :] = eps * (2.0 * scale)
         return 0
 
     lax.fori_loop(0, 2, look_up, 0)
 
-    for load in loads[1:]:
+    for load in loads[3:]:
         load.wait()
 
     def row_y(ref, i):
@@ -169,30 +197,36 @@
         )
 
     halos = [
-        remote(halo_mx_s, halo_mx, halo_send.at[0], halo_recv.at[0], at_row(up_r)),
+        remote(my.at[pl.ds(cells - ly, ly), :], halo_my, halo_send.at[0], halo_recv.at[0], at_col(up_c)),
         remote(halo_ez_s, halo_ez, halo_send.at[1], halo_recv.at[1], at_row(down_r)),
-        remote(my.at[pl.ds(cells - ly, ly), :], halo_my, halo_send.at[2], halo_recv.at[2], at_col(up_c)),
+        remote(halo_mx_s, halo_mx, halo_send.at[2], halo_recv.at[2], at_row(up_r)),
         remote(ex.at[pl.ds(0, ly), :], halo_ex, halo_send.at[3], halo_recv.at[3], at_col(down_c)),
     ]
     for halo in halos:
         halo.start()
 
-    def matrix_forward(n, row, first_gate, u_ref, r_ref, send, count):
-        diag = row(recip, 0) + (2.0 - first_gate)
-        inv = 1.0 / diag
+    def matrix_forward(n, row, gate, u_ref, r_ref, send, count):
+        share = row(recip, 0)
+        rest = share + gate
+        inv = 1.0 / (1.0 + rest)
         reach = inv
-        beta = reach
+        gain = share * inv
+        beta, gains = reach, gain
         u_ref[0], r_ref[0] = reach, inv
         for i in range(1, n - 1):
-            diag = row(recip, i) + 2.0 - inv
-            inv = 1.0 / diag
+            share = row(recip, i)
+            rest = share + rest * inv
+            inv = 1.0 / (1.0 + rest)
+            gain = (share + gain) * inv
+            gains = gains + reach * gain
             further = reach * inv
             beta = beta + reach * further
             reach = further
             u_ref[i], r_ref[i] = reach, inv
-        send[pl.ds(0, count, stride=TILE), :] = row(recip, n - 1) + 2.0 - inv
-        send[pl.ds(1, count, stride=TILE), :] = beta
+        send[pl.ds(0, count, stride=TILE), :] = row(recip, n - 1) + gain
+        send[pl.ds(1, count, stride=TILE), :] = gains
         send[pl.ds(2, count, stride=TILE), :] = reach
+        send[pl.ds(6, count, stride=TILE), :] = beta
 
     def rhs_forward(n, row, f_ref, u_ref, r_ref, v_ref, send, count, passed_on):
         value = row(f_ref, 0) * r_ref[0]
@@ -207,7 +241,7 @@
         send[pl.ds(5, count, stride=TILE), :] = passed_on
 
     def back(n, row_put, u_ref, r_ref, v_ref, got, count, out, diff):
-        before = got[pl.ds(0, count, stride=TILE), :] + got[pl.ds(3, count, stride=TILE), :]
+        before = got[pl.ds(0, count, stride=TILE), :]
         value = got[pl.ds(1, count, stride=TILE), :]
         row_put(out, n - 1, value)
         row_put(diff, n - 1, got[pl.ds(2, count, stride=TILE), :] - value)
@@ -217,23 +251,22 @@
             row_put(diff, i, value - lower)
             value = lower
 
-    first_r, first_c = 1.0 - gate_r, 1.0 - gate_c
-    matrix_forward(ly, row_y, first_r, uy, ry, send_y, lz)
-    matrix_forward(lz, row_z, first_c, uz, rz, send_z, ly)
+    matrix_forward(ly, row_y, gate_r, uy, ry, send_y0, lz)
+    matrix_forward(lz, row_z, gate_c, uz, rz, send_z0, ly)
 
     chunk = 32 if cells % 32 == 0 else 8
 
     def x_setup(c, _):
         at = pl.multiple_of(c * chunk, 8)
-        diag = recip[pl.ds(at, chunk), :]
-        lane = lax.broadcasted_iota(jnp.int32, diag.shape, 1)
+        excess = recip[pl.ds(at, chunk), :]
+        lane = lax.broadcasted_iota(jnp.int32, excess.shape, 1)
         low = jnp.where(lane == 0, 0.0, 1.0)
         up = jnp.where(lane == nx - 1, 0.0, 1.0)
 
         def keep(slot, values):
             xfac[slot, pl.ds(at, chunk), :] = values
 
-        cyclic_setup(low, up, diag + 1.0 + low, 1, keep)
+        cyclic_setup(low, up, excess + (1.0 - up), 1, keep)
         return 0
 
     lax.fori_loop(0, cells // chunk, x_setup, 0)
@@ -282,22 +315,12 @@
     ey_v = ey[...]
     ay_v = mz_v * inv_half - (after_x(ey_v) - ey_v)
     ay[...] = ay_v
-    for halo in halos:
-        halo.wait_recv()
+    halos[0].wait_recv()
     my_v = my[...]
     my_before = before_z(my_v, halo_my[...] * gate_c)
-    fx[...] = (
-        keepf[...] * ex[...] - (my_v - my_before) * inv_half + (ay_v - before_y(ay_v, zero_y, sh0))
-    )
-    ez_v = ez[...]
-    mx_v = mx[...]
-    ez_after = after_y(ez_v, halo_ez[pl.ds(0, lz), :] * gate_r_end, sh1)
-    az_v = mx_v * inv_half - (ez_after - ez_v)
-    az[...] = az_v
-    fy[...] = (
-        keepf[...] * ey_v - (mz_v - before_x(mz_v)) * inv_half + (az_v - before_z(az_v, zero_z))
-    )
-
+    gx_v = keepf[...] * ex[...] - (my_v - my_before) * inv_half
+    gx[...] = gx_v
+    fx[...] = gx_v + (ay_v - before_y(ay_v, zero_y, sh0))
     me_owner_j = lax.div(lz * me_r + nrow - 1, nrow)
 
     def owner_of(j):
@@ -305,6 +328,18 @@
 
     owns = jnp.logical_and(me_owner_j < lz, owner_of(me_owner_j) == me_r)
     others = jnp.logical_not(owns)
+
+    def for_each(count, body):
+        half = count // 2
+
+        def pair(k, _):
+            body(half + k, 0)
+            body(half - 1 - k, 0)
+            return 0
+
+        lax.fori_loop(0, half, pair, 0)
+        if count % 2:
+            body(count - 1, 0)
 
     def tile(ref, i):
         return ref.at[pl.ds(pl.multiple_of(i * TILE, TILE), TILE), :]
@@ -317,7 +352,11 @@
         part_of = ref.at[pl.ds(0, count * TILE), :]
         remote(part_of, part_of, sem, sem, at_row(up_r)).wait_recv()
 
+    sends_y, sends_z = (send_y0, send_y1), (send_z0, send_z1)
+
     def scatter_y(step):
+        send_y = sends_y[step]
+
         def to_owner(i, _):
             j = lax.rem(me_r + i, lz)
             owner = owner_of(j)
@@ -339,6 +378,8 @@
             ]
 
     def scatter_z(step):
+        send_z = sends_z[step]
+
         def to_owner(i, _):
             q = lax.rem(me_c + 1 + i, ncol)
             remote(
@@ -346,7 +387,7 @@
             ).start()
             return 0
 
-        lax.fori_loop(0, ncol - 1, to_owner, 0)
+        for_each(ncol - 1, to_owner)
         own = pl.ds(pl.multiple_of(me_c * TILE, TILE), TILE)
         gat_z[step, own, :] = send_z[own, :]
 
@@ -357,7 +398,7 @@
         place = lax.broadcasted_iota(jnp.int32, (n, nx), 0)
         starts, ends = place == 0, place == n - 1
         if step == 0:
-            beta = read(1)
+            beta = read(6)
             link = jnp.where(starts, 0.0, read(2))
             beta_up = jnp.where(ends, 0.0, roll(beta, n - 1, 0))
             link_up = jnp.where(ends, 0.0, roll(link, n - 1, 0))
@@ -366,7 +407,8 @@
             def keep(slot, values):
                 fac[slot] = values
 
-            cyclic_setup(link, link_up, read(0) - beta_up, 0, keep)
+            excess = read(0) + jnp.where(ends, 1.0, roll(read(1), n - 1, 0))
+            cyclic_setup(link, link_up, excess, 0, keep)
         else:
             beta, link, beta_up, link_up = mid[0], mid[1], mid[2], mid[3]
         added = jnp.where(starts, 0.0, roll(read(5), 1, 0))
@@ -374,12 +416,11 @@
         psi = read(4) + beta * added
         psi_up = jnp.where(ends, 0.0, roll(psi, n - 1, 0))
         last = cyclic_solve(phi + psi_up, 0, lambda slot: fac[slot])
-        before = jnp.where(starts, 0.0, roll(last, 1, 0))
+        before = jnp.where(starts, 0.0, roll(last, 1, 0)) + added
         after = psi_up + beta_up * last + link_up * roll(last, n - 1, 0)
         ret[step, pl.ds(0, n, stride=TILE), :] = before
         ret[step, pl.ds(1, n, stride=TILE), :] = last
         ret[step, pl.ds(2, n, stride=TILE), :] = after
-        ret[step, pl.ds(3, n, stride=TILE), :] = added
 
     def own_y(step):
         @pl.when(owns)
@@ -394,7 +435,7 @@
                 ).start()
                 return 0
 
-            lax.fori_loop(0, nrow - 1, give, 0)
+            for_each(nrow - 1, give)
             res_y[step, pl.ds(pl.multiple_of(me_owner_j * TILE, TILE), TILE), :] = ret_y[
                 step, pl.ds(pl.multiple_of(me_r * TILE, TILE), TILE), :
             ]
@@ -410,11 +451,13 @@
             ).start()
             return 0
 
-        lax.fori_loop(0, ncol - 1, give, 0)
+        for_each(ncol - 1, give)
         own = pl.ds(pl.multiple_of(me_c * TILE, TILE), TILE)
         res_z[step, own, :] = ret_z[step, own, :]
 
     def wait_sent(step):
+        send_y, send_z = sends_y[step], sends_z[step]
+
         @pl.when(owns)
         def _():
             wait_send(send_y, lz - 1, sems.at[0, step])
@@ -439,19 +482,30 @@
     def wait_z(step):
         wait_recv(res_z.at[step], ncol - 1, sems.at[7, step])
 
-    rhs_forward(ly, row_y, fx, uy, ry, vy, send_y, lz, -row_y(ay, ly - 1))
+    rhs_forward(ly, row_y, fx, uy, ry, vy, send_y0, lz, -row_y(ay, ly - 1))
     scatter_y(0)
-    rhs_forward(lz, row_z, fy, uz, rz, vz, send_z, ly, -row_z(az, lz - 1))
+    halos[1].wait_recv()
+    ez_v = ez[...]
+    mx_v = mx[...]
+    ez_after = after_y(ez_v, halo_ez[pl.ds(0, lz), :] * gate_r_end, sh1)
+    az_v = mx_v * inv_half - (ez_after - ez_v)
+    az[...] = az_v
+    gy_v = keepf[...] * ey_v - (mz_v - before_x(mz_v)) * inv_half
+    gy[...] = gy_v
+    fy[...] = gy_v + (az_v - before_z(az_v, zero_z))
+    rhs_forward(lz, row_z, fy, uz, rz, vz, send_z0, ly, -row_z(az, lz - 1))
     scatter_z(0)
 
+    halos[2].wait_recv()
+    halos[3].wait_recv()
     ex_v = ex[...]
     ax_v = my[...] * inv_half - (after_z(ex_v, halo_ex[...] * gate_c_end) - ex_v)
     ax[...] = ax_v
     mx_v = mx[...]
     mx_before = before_y(mx_v, halo_mx[pl.ds(0, lz), :] * gate_r, sh2)
-    fz[...] = (
-        keepf[...] * ez[...] - (mx_v - mx_before) * inv_half + (ax_v - before_x(ax_v))
-    )
+    gz_v = keepf[...] * ez[...] - (mx_v - mx_before) * inv_half
+    gz[...] = gz_v
+    fz[...] = gz_v + (ax_v - before_x(ax_v))
 
     def keep_half(at, solved, ahead):
         ez1[at, :] = solved
@@ -460,59 +514,65 @@
     x_solve(fz, keep_half)
     cz_v = ax[...] + 2.0 * dez[...]
     cz[...] = cz_v
-    hy_v = ax[...] + dez[...]
-    fz[...] = keepf[...] * ez1[...] + (hy_v - before_x(hy_v))
-    fx[...] = before_z(cz_v, zero_z) - cz_v
+    fz[...] = twice[...] * ez1[...] - gz[...]
+    fx[...] = (before_z(cz_v, zero_z) - cz_v) - gx[...]
 
     own_z(0)
     own_y(0)
-    wait_sent(0)
-
     wait_z(0)
     back(lz, put_z, uz, rz, vz, res_z.at[0], ly, ey1, dey)
     wait_y(0)
     back(ly, put_y, uy, ry, vy, res_y.at[0], lz, ex1, dex)
 
-    dex_v, dey_v = dex[...], dey[...]
-    ay_v, az_v = ay[...], az[...]
-    cx_v, cy_v = ay_v + 2.0 * dex_v, az_v + 2.0 * dey_v
+    cx_v = ay[...] + 2.0 * dex[...]
+    cy_v = az[...] + 2.0 * dey[...]
     cx[...], cy[...] = cx_v, cy_v
-    hz_v = ay_v + dex_v
-    hz_first = (
-        row_y(ex1, 0) - res_y[0, pl.ds(0, lz, stride=TILE), :] - res_y[0, pl.ds(3, lz, stride=TILE), :]
-    ) * gate_r
-    fx[...] = fx[...] + keepf[...] * ex1[...] + (hz_v - before_y(hz_v, hz_first, sh0))
     fz[...] = fz[...] - (cy_v - before_y(cy_v, zero_y, sh1))
-
-    rhs_forward(ly, row_y, fz, uy, ry, vy, send_y, lz, row_y(cy, ly - 1))
+    fx[...] = fx[...] + twice[...] * ex1[...]
+
+    rhs_forward(ly, row_y, fz, uy, ry, vy, send_y1, lz, row_y(cy, ly - 1))
     scatter_y(1)
-    rhs_forward(lz, row_z, fx, uz, rz, vz, send_z, ly, row_z(cz, lz - 1))
+    rhs_forward(lz, row_z, fx, uz, rz, vz, send_z1, ly, row_z(cz, lz - 1))
     scatter_z(1)
 
-    hx_v = az[...] + dey[...]
-    hx_first = (
-        row_z(ey1, 0) - res_z[0, pl.ds(0, ly, stride=TILE), :] - res_z[0, pl.ds(3, ly, stride=TILE), :]
-    ) * gate_c
     cx_v = cx[...]
-    fy[...] = keepf[...] * ey1[...] + (hx_v - before_z(hx_v, hx_first)) - (cx_v - before_x(cx_v))
+    fy[...] = (twice[...] * ey1[...] - gy[...]) - (cx_v - before_x(cx_v))
 
     def write_y(at, solved, ahead):
         ney[at, :] = solved
         nhz[at, :] = (cx[at, :] - ahead) * half_step
 
     x_solve(fy, write_y)
+    store(1, 5)
 
     own_z(1)
     own_y(1)
     wait_z(1)
     back(lz, put_z, uz, rz, vz, res_z.at[1], ly, nex, dez)
     nhy[...] = (cz[...] - dez[...]) * half_step
+    store(0, 4)
     wait_y(1)
     back(ly, put_y, uy, ry, vy, res_y.at[1], lz, nez, dex)
     nhx[...] = (cy[...] - dex[...]) * half_step
+    store(2, 3)
+    wait_sent(0)
     wait_sent(1)
     for halo in halos:
         halo.wait_send()
+    for done in stores:
+        done.wait()
+
+
+def deliver(*refs):
+    sem = refs[12]
+    copies = [
+        pltpu.make_async_copy(src, dst, sem.at[i])
+        for i, (src, dst) in enumerate(zip(refs[:6], refs[6:12]))
+    ]
+    for copy in copies:
+        copy.start()
+    for copy in copies:
+        copy.wait()
 
 
 def solution(mesh):
@@ -527,13 +587,14 @@
         pad_z = -(-lz // 8) * 8
         slots = lambda n: 2 * levels_of(n) + 1
         scratch = (
-            [whole] * 6
+            [pltpu.SMEM((nt,), f32)] * 2
+            + [whole] * 6
             + [pltpu.VMEM((cells, nx), jnp.int32)]
-            + [whole] * 21
+            + [whole] * 31
             + [pltpu.VMEM((slots(nx), cells, nx), f32)]
             + [pltpu.VMEM((ly - 1, lz, nx), f32)] * 3
             + [pltpu.VMEM((lz - 1, ly, nx), f32)] * 3
-            + [pltpu.VMEM((lz * TILE, nx), f32), pltpu.VMEM((ly * TILE, nx), f32)]
+            + [pltpu.VMEM((lz * TILE, nx), f32)] * 2 + [pltpu.VMEM((ly * TILE, nx), f32)] * 2
             + [pltpu.VMEM((2, nrow * TILE, nx), f32), pltpu.VMEM((2, ncol * TILE, nx), f32)] * 2
             + [pltpu.VMEM((2, lz * TILE, nx), f32), pltpu.VMEM((2, ly * TILE, nx), f32)]
             + [pltpu.VMEM((slots(nrow), nrow, nx), f32), pltpu.VMEM((slots(ncol), ncol, nx), f32)]
@@ -541,7 +602,8 @@
             + [pltpu.VMEM((pad_z, nx), f32)] * 4
             + [pltpu.VMEM((ly, nx), f32)] * 2
             + [
-                pltpu.SemaphoreType.DMA((7,)),
+                pltpu.SemaphoreType.DMA((9,)),
+                pltpu.SemaphoreType.DMA((6,)),
                 pltpu.SemaphoreType.DMA((4,)),
                 pltpu.SemaphoreType.DMA((4,)),
                 pltpu.SemaphoreType.DMA((8, 2)),
@@ -550,13 +612,21 @@
         outs = pl.pallas_call(
             functools.partial(kernel, (lz, ly, nx, nrow, ncol, nt)),
             out_shape=[jax.ShapeDtypeStruct((cells, nx), f32)] * 6,
-            in_specs=[pl.BlockSpec(memory_space=pl.ANY)] * 7 + [pl.BlockSpec(memory_space=pltpu.SMEM)] * 2,
-            out_specs=[pl.BlockSpec(memory_space=pltpu.VMEM)] * 6,
+            in_specs=[pl.BlockSpec(memory_space=pltpu.HBM)] * 9,
+            out_specs=[pl.BlockSpec(memory_space=pltpu.HBM)] * 6,
             scratch_shapes=scratch,
             compiler_params=pltpu.CompilerParams(
-                collective_id=0, has_side_effects=True, vmem_limit_bytes=32 * 1024 * 1024
+                collective_id=0, has_side_effects=True, vmem_limit_bytes=VMEM_BYTES
             ),
         )(*flat, permittivity, conductivity)
+        outs = pl.pallas_call(
+            deliver,
+            out_shape=[jax.ShapeDtypeStruct((cells, nx), f32)] * 6,
+            in_specs=[pl.BlockSpec(memory_space=pltpu.HBM)] * 6,
+            out_specs=[pl.BlockSpec(memory_space=pltpu.HBM)] * 6,
+            scratch_shapes=[pltpu.SemaphoreType.DMA((6,))],
+            compiler_params=pltpu.CompilerParams(vmem_limit_bytes=VMEM_BYTES),
+        )(*outs)
         return tuple(o.reshape(lz, ly, nx) for o in outs)
 
     cut = P("col", "row", None)

time: 59 us -> 66 us (1.12)
  Pallas kernels: 47.3 us -> 65.2 us
  local copies, waits for them, and re-layouts: 10.7 us -> 0 us
    pallas_call x0 -> x1, Pallas kernels: none -> 19 us  [per_device(): pl.pallas_call(deliver, out_shape=[jax.ShapeDtypeStruct((cells, nx), f32)...]
    unnamed x24 -> x0, local copies, waits for them, and re-layouts: 10.7 us -> none
    pallas_call x1, Pallas kernels: 47.3 us -> 46.2 us  [per_device(): pl.pallas_call(functools.partial(kernel, (lz, ly, nx, nrow, ncol, nt)), o...]
where the time goes in v1:
time: 66 us; the launch traced here: 65.9 us
  Pallas kernels  65.2 us (99%)
    pallas_call x1, Pallas kernels, per_device(): pl.pallas_call(functools.partial(kernel, (lz, ly, nx, nrow, ncol, nt)), o...  46.2 us
    pallas_call x1, Pallas kernels, per_device(): pl.pallas_call(deliver, out_shape=[jax.ShapeDtypeStruct((cells, nx), f32)...  19 us

profile of v1, /device:TPU:1, one launch (start us, length us, event | category | flops | bytes accessed | tf_op | source)
XLA Modules:
  0.0 65.9 jit_solution(14003172751561344754)
XLA Ops:
  0.6 46.2 %shard_map.136 = (f32[192,128]{1,0:T(8,128)}, f32[192,128]{1,0:T(8,128)}, f32[192,128]{1,0:T(8,128)}, f32[192,128]{1,0:T(8,128)}, f32[192,128]{1,0:T(8,128)}, /*index=5*/f32[192,128]{1,0:T(8,128)}) custom-call(f32[192,128]{1,0:T(8,128)} %bitcast.13, f32[192,128]{1,0:T(8,128)} %bitcast.14, f32[192,128]{1,0:T(8,128)} %bitcast.15, f32[192,128]{1,0:T(8,128)} %bitcast.16, ...), custom_call_target="tpu_custom_call" | custom-call | tf_op jit(solution)/shard_map/pallas_call | solution.py:612
  46.9 19.0 %shard_map.137 = (f32[192,128]{1,0:T(8,128)}, f32[192,128]{1,0:T(8,128)}, f32[192,128]{1,0:T(8,128)}, f32[192,128]{1,0:T(8,128)}, f32[192,128]{1,0:T(8,128)}, /*index=5*/f32[192,128]{1,0:T(8,128)}) custom-call(f32[192,128]{1,0:T(8,128)} %get-tuple-element.18.refs_0_, f32[192,128]{1,0:T(8,128)} %get-tuple-element.19.refs_1_, ...), custom_call_target="tpu_custom_call" | custom-call | tf_op jit(solution)/shard_map/pallas_call | solution.py:622

commit v2 on v1

v2 whole, which is shorter than its diff:
```python
import functools

import jax
import jax.numpy as jnp
from jax import lax
from jax.experimental import pallas as pl
from jax.experimental.pallas import tpu as pltpu
from jax.sharding import PartitionSpec as P

MESH = pl.DeviceIdType.MESH
half_step = 32.0
inv_half = 1.0 / half_step
TILE = 4
VMEM_BYTES = 56 * 1024 * 1024


def roll(values, shift, axis):
    return pltpu.roll(values, shift, axis)


def cyclic_setup(low, up, excess, axis, keep):
    n = excess.shape[axis]
    stride = 1
    level = 0
    while stride < n:
        inv = 1.0 / (low + up + excess)
        from_low = low * roll(inv, stride, axis)
        from_up = up * roll(inv, n - stride, axis)
        excess = (
            excess
            + from_low * roll(excess, stride, axis)
            + from_up * roll(excess, n - stride, axis)
        )
        if 2 * stride < n:
            low = from_low * roll(low, stride, axis)
            up = from_up * roll(up, n - stride, axis)
        keep(2 * level, from_low)
        keep(2 * level + 1, from_up)
        stride, level = 2 * stride, level + 1
    keep(2 * level, 1.0 / excess)


def cyclic_solve(rhs, axis, kept):
    n = rhs.shape[axis]
    stride = 1
    level = 0
    while stride < n:
        rhs = (
            rhs
            + kept(2 * level) * roll(rhs, stride, axis)
            + kept(2 * level + 1) * roll(rhs, n - stride, axis)
        )
        stride, level = 2 * stride, level + 1
    return rhs * kept(2 * level)


def levels_of(n):
    return (n - 1).bit_length()


def kernel(sizes, *refs):
    lz, ly, nx, nrow, ncol, nt = sizes
    cells = lz * ly
    (ex_h, ey_h, ez_h, mx_h, my_h, mz_h, tis_h, eps_h, sig_h) = refs[:9]
    outs_h = refs[9:15]
    (
        eps_s, sig_s,
        ex, ey, ez, mx, my, mz, tis,
        nex, ney, nez, nhx, nhy, nhz,
        recip, keepf, twice, gx, gy, gz, ax, ay, az,
        fx, fy, fz, ex1, ey1, ez1, dex, dey, dez, cx, cy, cz,
        sh0, sh1, sh2, sh3,
        xfac,
        uy, ry, vy, uz, rz, vz,
        send_y0, send_y1, send_ym, send_z0, send_z1, send_zm, gat_y, gat_z, ret_y, ret_z, res_y, res_z,
        fac_y, fac_z, mid_y, mid_z,
        halo_mx_s, halo_ez_s, halo_mx, halo_ez, halo_my, halo_ex,
        load_sem, store_sem, halo_send, halo_recv, sems,
    ) = refs[15:]

    me_r, me_c = lax.axis_index("row"), lax.axis_index("col")
    gate_r = jnp.where(me_r > 0, 1.0, 0.0)
    gate_c = jnp.where(me_c > 0, 1.0, 0.0)
    gate_r_end = jnp.where(me_r < nrow - 1, 1.0, 0.0)
    gate_c_end = jnp.where(me_c < ncol - 1, 1.0, 0.0)

    def at_row(p):
        return (p, me_c)

    def at_col(p):
        return (me_r, p)

    loads = [
        pltpu.make_async_copy(src, dst, load_sem.at[i])
        for i, (src, dst) in enumerate(
            (
                (eps_h, eps_s),
                (sig_h, sig_s),
                (tis_h, tis),
                (mx_h, mx),
                (ez_h, ez),
                (my_h, my),
                (ex_h, ex),
                (ey_h, ey),
                (mz_h, mz),
            )
        )
    ]
    for load in loads:
        load.start()

    stores = [
        pltpu.make_async_copy(src, dst, store_sem.at[i])
        for i, (src, dst) in enumerate(zip((nex, ney, nez, nhx, nhy, nhz), outs_h))
    ]

    def store(*which):
        for i in which:
            stores[i].start()

    barrier = pltpu.get_barrier_semaphore()

    def greet_row(i, _):
        pl.semaphore_signal(
            barrier, inc=1, device_id=at_row(lax.rem(me_r + 1 + i, nrow)), device_id_type=MESH
        )
        return 0

    def greet_col(i, _):
        pl.semaphore_signal(
            barrier, inc=1, device_id=at_col(lax.rem(me_c + 1 + i, ncol)), device_id_type=MESH
        )
        return 0

    lax.fori_loop(0, nrow - 1, greet_row, 0)
    lax.fori_loop(0, ncol - 1, greet_col, 0)

    for load in loads[:3]:
        load.wait()
    part = cells // 2
    group = 4

    def look_up(c, _):
        at = pl.ds(pl.multiple_of(c * part, 8), part)
        label = tis[at, :]

        def tissues(g, carry):
            eps, sig = carry
            for j in range(group):
                t = g * group + j
                same = label == t
                eps = jnp.where(same, eps_s[t], eps)
                sig = jnp.where(same, sig_s[t], sig)
            return eps, sig

        zero = jnp.zeros(label.shape, jnp.float32)
        eps, sig = lax.fori_loop(0, nt // group, tissues, (zero, zero))
        loss = sig * (0.5 * half_step)
        scale = inv_half * inv_half
        recip[at, :] = (eps + loss) * scale
        keepf[at, :] = (eps - loss) * scale
        twice[at, :] = eps * (2.0 * scale)
        return 0

    lax.fori_loop(0, 2, look_up, 0)

    for load in loads[3:]:
        load.wait()

    def row_y(ref, i):
        return ref[pl.ds(i, lz, stride=ly), :]

    def put_y(ref, i, values):
        ref[pl.ds(i, lz, stride=ly), :] = values

    def row_z(ref, i):
        return ref[pl.ds(i * ly, ly), :]

    def put_z(ref, i, values):
        ref[pl.ds(i * ly, ly), :] = values

    def matrix_forward(n, row, gate, u_ref, r_ref, send):
        share = row(recip, 0)
        rest = share + gate
        inv = 1.0 / (1.0 + rest)
        reach = inv
        gain = share * inv
        beta, gains = reach, gain
        u_ref[0], r_ref[0] = reach, inv
        for i in range(1, n - 1):
            share = row(recip, i)
            rest = share + rest * inv
            inv = 1.0 / (1.0 + rest)
            gain = (share + gain) * inv
            gains = gains + reach * gain
            further = reach * inv
            beta = beta + reach * further
            reach = further
            u_ref[i], r_ref[i] = reach, inv
        send[:, 0, :] = row(recip, n - 1) + gain
        send[:, 1, :] = gains
        send[:, 2, :] = reach
        send[:, 3, :] = beta

    matrix_forward(ly, row_y, gate_r, uy, ry, send_ym)
    matrix_forward(lz, row_z, gate_c, uz, rz, send_zm)

    halo_mx_s[pl.ds(0, lz), :] = row_y(mx, ly - 1)
    halo_ez_s[pl.ds(0, lz), :] = row_y(ez, 0)
    pl.semaphore_wait(barrier, nrow + ncol - 2)

    up_r, down_r = lax.rem(me_r + 1, nrow), lax.rem(me_r + nrow - 1, nrow)
    up_c, down_c = lax.rem(me_c + 1, ncol), lax.rem(me_c + ncol - 1, ncol)

    def remote(src, dst, send_sem, recv_sem, device):
        return pltpu.make_async_remote_copy(
            src_ref=src,
            dst_ref=dst,
            send_sem=send_sem,
            recv_sem=recv_sem,
            device_id=device,
            device_id_type=MESH,
        )

    halos = [
        remote(my.at[pl.ds(cells - ly, ly), :], halo_my, halo_send.at[0], halo_recv.at[0], at_col(up_c)),
        remote(halo_ez_s, halo_ez, halo_send.at[1], halo_recv.at[1], at_row(down_r)),
        remote(halo_mx_s, halo_mx, halo_send.at[2], halo_recv.at[2], at_row(up_r)),
        remote(ex.at[pl.ds(0, ly), :], halo_ex, halo_send.at[3], halo_recv.at[3], at_col(down_c)),
    ]
    for halo in halos:
        halo.start()

    def rhs_forward(n, row, f_ref, u_ref, r_ref, v_ref, send, passed_on):
        value = row(f_ref, 0) * r_ref[0]
        psi = value
        v_ref[0] = value
        for i in range(1, n - 1):
            value = (row(f_ref, i) + value) * r_ref[i]
            psi = psi + u_ref[i - 1] * value
            v_ref[i] = value
        send[:, 0, :] = row(f_ref, n - 1) + value
        send[:, 1, :] = psi
        send[:, 2, :] = passed_on

    def back(n, row_put, u_ref, r_ref, v_ref, got, out, diff):
        before = got[:, 0, :]
        value = got[:, 1, :]
        row_put(out, n - 1, value)
        row_put(diff, n - 1, got[:, 2, :] - value)
        for i in range(n - 2, -1, -1):
            lower = (v_ref[i] + u_ref[i] * before) + r_ref[i] * value
            row_put(out, i, lower)
            row_put(diff, i, value - lower)
            value = lower


    me_owner_j = lax.div(lz * me_r + nrow - 1, nrow)

    def owner_of(j):
        return lax.div(j * nrow, lz)

    owns = jnp.logical_and(me_owner_j < lz, owner_of(me_owner_j) == me_r)
    others = jnp.logical_not(owns)

    def for_each(count, body):
        half = count // 2

        def pair(k, _):
            body(half + k, 0)
            body(half - 1 - k, 0)
            return 0

        lax.fori_loop(0, half, pair, 0)
        if count % 2:
            body(count - 1, 0)

    def tile(ref, i):
        return ref.at[i]

    def wait_send(ref, count, sem):
        part_of = ref.at[pl.ds(0, count)]
        remote(part_of, part_of, sem, sem, at_row(up_r)).wait_send()

    def wait_recv(ref, count, sem):
        part_of = ref.at[pl.ds(0, count)]
        remote(part_of, part_of, sem, sem, at_row(up_r)).wait_recv()

    sends_y, sends_z = (send_y0, send_y1, send_ym), (send_z0, send_z1, send_zm)

    def scatter_y(step):
        send_y = sends_y[step]

        def to_owner(i, _):
            j = lax.rem(me_r + i, lz)
            owner = owner_of(j)

            @pl.when(owner != me_r)
            def _():
                remote(
                    tile(send_y, j), tile(gat_y.at[step], me_r), sems.at[0, step], sems.at[1, step], at_row(owner)
                ).start()

            return 0

        lax.fori_loop(0, lz, to_owner, 0)

        @pl.when(owns)
        def _():
            gat_y[step, me_r] = send_y[me_owner_j]

    def scatter_z(step):
        send_z = sends_z[step]

        def to_owner(i, _):
            q = lax.rem(me_c + 1 + i, ncol)
            remote(
                tile(send_z, q), tile(gat_z.at[step], me_c), sems.at[2, step], sems.at[3, step], at_col(q)
            ).start()
            return 0

        for_each(ncol - 1, to_owner)
        gat_z[step, me_c] = send_z[me_c]

    def factor_owned(n, got, fac, mid):
        def read(r):
            return got[2, :, r, :]

        place = lax.broadcasted_iota(jnp.int32, (n, nx), 0)
        starts, ends = place == 0, place == n - 1
        beta = read(3)
        link = jnp.where(starts, 0.0, read(2))
        beta_up = jnp.where(ends, 0.0, roll(beta, n - 1, 0))
        link_up = jnp.where(ends, 0.0, roll(link, n - 1, 0))
        mid[0], mid[1], mid[2], mid[3] = beta, link, beta_up, link_up

        def keep(slot, values):
            fac[slot] = values

        excess = read(0) + jnp.where(ends, 1.0, roll(read(1), n - 1, 0))
        cyclic_setup(link, link_up, excess, 0, keep)

    def solve_owned(step, n, got, fac, mid, ret):
        def read(r):
            return got[step, :, r, :]

        place = lax.broadcasted_iota(jnp.int32, (n, nx), 0)
        starts, ends = place == 0, place == n - 1
        beta, link, beta_up, link_up = mid[0], mid[1], mid[2], mid[3]
        added = jnp.where(starts, 0.0, roll(read(2), 1, 0))
        phi = read(0) + link * added
        psi = read(1) + beta * added
        psi_up = jnp.where(ends, 0.0, roll(psi, n - 1, 0))
        last = cyclic_solve(phi + psi_up, 0, lambda slot: fac[slot])
        before = jnp.where(starts, 0.0, roll(last, 1, 0)) + added
        after = psi_up + beta_up * last + link_up * roll(last, n - 1, 0)
        ret[step, :, 0, :] = before
        ret[step, :, 1, :] = last
        ret[step, :, 2, :] = after

    def own_factors():
        wait_recv(gat_z.at[2], ncol - 1, sems.at[3, 2])
        factor_owned(ncol, gat_z, fac_z, mid_z)

        @pl.when(owns)
        def _():
            wait_recv(gat_y.at[2], nrow - 1, sems.at[1, 2])
            factor_owned(nrow, gat_y, fac_y, mid_y)

    def own_y(step):
        @pl.when(owns)
        def _():
            wait_recv(gat_y.at[step], nrow - 1, sems.at[1, step])
            solve_owned(step, nrow, gat_y, fac_y, mid_y, ret_y)

            def give(i, _):
                q = lax.rem(me_r + 1 + i, nrow)
                remote(
                    tile(ret_y.at[step], q), tile(res_y.at[step], me_owner_j), sems.at[4, step], sems.at[5, step], at_row(q)
                ).start()
                return 0

            for_each(nrow - 1, give)
            res_y[step, me_owner_j] = ret_y[step, me_r]

    def own_z(step):
        wait_recv(gat_z.at[step], ncol - 1, sems.at[3, step])
        solve_owned(step, ncol, gat_z, fac_z, mid_z, ret_z)

        def give(i, _):
            q = lax.rem(me_c + 1 + i, ncol)
            remote(
                tile(ret_z.at[step], q), tile(res_z.at[step], me_c), sems.at[6, step], sems.at[7, step], at_col(q)
            ).start()
            return 0

        for_each(ncol - 1, give)
        res_z[step, me_c] = ret_z[step, me_c]

    def wait_sent(step):
        send_y, send_z = sends_y[step], sends_z[step]

        @pl.when(owns)
        def _():
            wait_send(send_y, lz - 1, sems.at[0, step])
            if step < 2:
                wait_send(ret_y.at[step], nrow - 1, sems.at[4, step])

        @pl.when(others)
        def _():
            wait_send(send_y, lz, sems.at[0, step])

        wait_send(send_z, ncol - 1, sems.at[2, step])
        if step < 2:
            wait_send(ret_z.at[step], ncol - 1, sems.at[6, step])

    def wait_y(step):
        @pl.when(owns)
        def _():
            wait_recv(res_y.at[step], lz - 1, sems.at[5, step])

        @pl.when(others)
        def _():
            wait_recv(res_y.at[step], lz, sems.at[5, step])

    def wait_z(step):
        wait_recv(res_z.at[step], ncol - 1, sems.at[7, step])

    scatter_y(2)
    scatter_z(2)

    chunk = 32 if cells % 32 == 0 else 8

    def x_setup(c, _):
        at = pl.multiple_of(c * chunk, 8)
        excess = recip[pl.ds(at, chunk), :]
        lane = lax.broadcasted_iota(jnp.int32, excess.shape, 1)
        low = jnp.where(lane == 0, 0.0, 1.0)
        up = jnp.where(lane == nx - 1, 0.0, 1.0)

        def keep(slot, values):
            xfac[slot, pl.ds(at, chunk), :] = values

        cyclic_setup(low, up, excess + (1.0 - up), 1, keep)
        return 0

    lax.fori_loop(0, cells // chunk, x_setup, 0)

    lane = lax.broadcasted_iota(jnp.int32, (cells, nx), 1)

    def before_x(values):
        return jnp.where(lane == 0, 0.0, roll(values, 1, 1))

    def after_x(values):
        return jnp.where(lane == nx - 1, 0.0, roll(values, nx - 1, 1))

    def before_y(values, first, shifted):
        shifted[...] = roll(values, 1, 0)
        put_y(shifted, 0, first)
        return shifted[...]

    def after_y(values, last, shifted):
        shifted[...] = roll(values, cells - 1, 0)
        put_y(shifted, ly - 1, last)
        return shifted[...]

    def before_z(values, first):
        return jnp.concatenate([first, values[: cells - ly]], axis=0)

    def after_z(values, last):
        return jnp.concatenate([values[ly:], last], axis=0)

    def x_solve(f_ref, write):
        def lines(c, _):
            at = pl.multiple_of(c * chunk, 8)
            solved = cyclic_solve(
                f_ref[pl.ds(at, chunk), :], 1, lambda slot: xfac[slot, pl.ds(at, chunk), :]
            )
            column = lax.broadcasted_iota(jnp.int32, solved.shape, 1)
            ahead = jnp.where(column == nx - 1, 0.0, roll(solved, nx - 1, 1)) - solved
            write(pl.ds(at, chunk), solved, ahead)
            return 0

        lax.fori_loop(0, cells // chunk, lines, 0)

    zero_y = jnp.zeros((lz, nx), jnp.float32)
    zero_z = jnp.zeros((ly, nx), jnp.float32)

    mz_v = mz[...]
    ey_v = ey[...]
    ay_v = mz_v * inv_half - (after_x(ey_v) - ey_v)
    ay[...] = ay_v
    halos[0].wait_recv()
    my_v = my[...]
    my_before = before_z(my_v, halo_my[...] * gate_c)
    gx_v = keepf[...] * ex[...] - (my_v - my_before) * inv_half
    gx[...] = gx_v
    fx[...] = gx_v + (ay_v - before_y(ay_v, zero_y, sh0))
    rhs_forward(ly, row_y, fx, uy, ry, vy, send_y0, -row_y(ay, ly - 1))
    scatter_y(0)
    halos[1].wait_recv()
    ez_v = ez[...]
    mx_v = mx[...]
    ez_after = after_y(ez_v, halo_ez[pl.ds(0, lz), :] * gate_r_end, sh1)
    az_v = mx_v * inv_half - (ez_after - ez_v)
    az[...] = az_v
    gy_v = keepf[...] * ey_v - (mz_v - before_x(mz_v)) * inv_half
    gy[...] = gy_v
    fy[...] = gy_v + (az_v - before_z(az_v, zero_z))
    rhs_forward(lz, row_z, fy, uz, rz, vz, send_z0, -row_z(az, lz - 1))
    scatter_z(0)

    own_factors()
    halos[2].wait_recv()
    halos[3].wait_recv()
    ex_v = ex[...]
    ax_v = my[...] * inv_half - (after_z(ex_v, halo_ex[...] * gate_c_end) - ex_v)
    ax[...] = ax_v
    mx_v = mx[...]
    mx_before = before_y(mx_v, halo_mx[pl.ds(0, lz), :] * gate_r, sh2)
    gz_v = keepf[...] * ez[...] - (mx_v - mx_before) * inv_half
    gz[...] = gz_v
    fz[...] = gz_v + (ax_v - before_x(ax_v))

    def keep_half(at, solved, ahead):
        ez1[at, :] = solved
        dez[at, :] = ahead

    x_solve(fz, keep_half)
    cz_v = ax[...] + 2.0 * dez[...]
    cz[...] = cz_v
    fz[...] = twice[...] * ez1[...] - gz[...]
    fx[...] = (before_z(cz_v, zero_z) - cz_v) - gx[...]

    own_z(0)
    own_y(0)
    wait_z(0)
    back(lz, put_z, uz, rz, vz, res_z.at[0], ey1, dey)
    wait_y(0)
    back(ly, put_y, uy, ry, vy, res_y.at[0], ex1, dex)

    cx_v = ay[...] + 2.0 * dex[...]
    cy_v = az[...] + 2.0 * dey[...]
    cx[...], cy[...] = cx_v, cy_v
    fz[...] = fz[...] - (cy_v - before_y(cy_v, zero_y, sh1))
    fx[...] = fx[...] + twice[...] * ex1[...]

    rhs_forward(ly, row_y, fz, uy, ry, vy, send_y1, row_y(cy, ly - 1))
    scatter_y(1)
    rhs_forward(lz, row_z, fx, uz, rz, vz, send_z1, row_z(cz, lz - 1))
    scatter_z(1)

    cx_v = cx[...]
    fy[...] = (twice[...] * ey1[...] - gy[...]) - (cx_v - before_x(cx_v))

    def write_y(at, solved, ahead):
        ney[at, :] = solved
        nhz[at, :] = (cx[at, :] - ahead) * half_step

    x_solve(fy, write_y)
    store(1, 5)

    own_z(1)
    own_y(1)
    wait_z(1)
    back(lz, put_z, uz, rz, vz, res_z.at[1], nex, dez)
    nhy[...] = (cz[...] - dez[...]) * half_step
    store(0, 4)
    wait_y(1)
    back(ly, put_y, uy, ry, vy, res_y.at[1], nez, dex)
    nhx[...] = (cy[...] - dex[...]) * half_step
    store(2, 3)
    for step in range(3):
        wait_sent(step)
    for halo in halos:
        halo.wait_send()
    for done in stores:
        done.wait()


def deliver(*refs):
    made, placed, held = refs[:6], refs[6:12], refs[12:18]
    in_sem, out_sem = refs[18], refs[19]
    fetches = [
        pltpu.make_async_copy(made[i], held[i], in_sem.at[i]) for i in range(6)
    ]
    puts = [
        pltpu.make_async_copy(held[i], placed[i], out_sem.at[i]) for i in range(6)
    ]
    for fetch in fetches:
        fetch.start()
    for fetch, put in zip(fetches, puts):
        fetch.wait()
        put.start()
    for put in puts:
        put.wait()


def solution(mesh):
    nrow, ncol = mesh.shape["row"], mesh.shape["col"]

    def per_device(ex, ey, ez, mx, my, mz, tissue, permittivity, conductivity):
        lz, ly, nx = ex.shape
        cells, nt = lz * ly, permittivity.shape[0]
        f32 = jnp.float32
        flat = [a.reshape(cells, nx) for a in (ex, ey, ez, mx, my, mz, tissue)]
        whole = pltpu.VMEM((cells, nx), f32)
        pad_z = -(-lz // 8) * 8
        slots = lambda n: 2 * levels_of(n) + 1
        scratch = (
            [pltpu.SMEM((nt,), f32)] * 2
            + [whole] * 6
            + [pltpu.VMEM((cells, nx), jnp.int32)]
            + [whole] * 31
            + [pltpu.VMEM((slots(nx), cells, nx), f32)]
            + [pltpu.VMEM((ly - 1, lz, nx), f32)] * 3
            + [pltpu.VMEM((lz - 1, ly, nx), f32)] * 3
            + [pltpu.VMEM((lz, TILE, nx), f32)] * 3 + [pltpu.VMEM((ly, TILE, nx), f32)] * 3
            + [pltpu.VMEM((3, nrow, TILE, nx), f32), pltpu.VMEM((3, ncol, TILE, nx), f32)]
            + [pltpu.VMEM((2, nrow, TILE, nx), f32), pltpu.VMEM((2, ncol, TILE, nx), f32)]
            + [pltpu.VMEM((2, lz, TILE, nx), f32), pltpu.VMEM((2, ly, TILE, nx), f32)]
            + [pltpu.VMEM((slots(nrow), nrow, nx), f32), pltpu.VMEM((slots(ncol), ncol, nx), f32)]
            + [pltpu.VMEM((4, nrow, nx), f32), pltpu.VMEM((4, ncol, nx), f32)]
            + [pltpu.VMEM((pad_z, nx), f32)] * 4
            + [pltpu.VMEM((ly, nx), f32)] * 2
            + [
                pltpu.SemaphoreType.DMA((9,)),
                pltpu.SemaphoreType.DMA((6,)),
                pltpu.SemaphoreType.DMA((4,)),
                pltpu.SemaphoreType.DMA((4,)),
                pltpu.SemaphoreType.DMA((8, 3)),
            ]
        )
        outs = pl.pallas_call(
            functools.partial(kernel, (lz, ly, nx, nrow, ncol, nt)),
            out_shape=[jax.ShapeDtypeStruct((cells, nx), f32)] * 6,
            in_specs=[pl.BlockSpec(memory_space=pltpu.HBM)] * 9,
            out_specs=[pl.BlockSpec(memory_space=pltpu.HBM)] * 6,
            scratch_shapes=scratch,
            compiler_params=pltpu.CompilerParams(
                collective_id=0, has_side_effects=True, vmem_limit_bytes=VMEM_BYTES
            ),
        )(*flat, permittivity, conductivity)
        outs = pl.pallas_call(
            deliver,
            out_shape=[jax.ShapeDtypeStruct((cells, nx), f32)] * 6,
            in_specs=[pl.BlockSpec(memory_space=pltpu.HBM)] * 6,
            out_specs=[pl.BlockSpec(memory_space=pltpu.HBM)] * 6,
            scratch_shapes=[whole] * 6 + [pltpu.SemaphoreType.DMA((6,))] * 2,
            compiler_params=pltpu.CompilerParams(vmem_limit_bytes=VMEM_BYTES),
        )(*outs)
        return tuple(o.reshape(lz, ly, nx) for o in outs)

    cut = P("col", "row", None)
    return jax.shard_map(
        per_device,
        mesh=mesh,
        in_specs=(cut,) * 7 + (P(), P()),
        out_specs=(cut,) * 6,
        check_vma=False,
    )
```

time: 66 us -> 47.5 us (0.72)
  Pallas kernels: 65.2 us -> 46.7 us
    pallas_call x1, Pallas kernels: 19 us -> 1.88 us  [per_device(): pl.pallas_call(deliver, out_shape=[jax.ShapeDtypeStruct((cells, nx), f32)...]
    pallas_call x1, Pallas kernels: 46.2 us -> 44.8 us  [per_device(): pl.pallas_call(functools.partial(kernel, (lz, ly, nx, nrow, ncol, nt)), o...]
where the time goes in v2:
time: 47.5 us; the launch traced here: 47.3 us
  Pallas kernels  46.7 us (98%)
  between operations  0.64 us (1%)
    pallas_call x1, Pallas kernels, per_device(): pl.pallas_call(functools.partial(kernel, (lz, ly, nx, nrow, ncol, nt)), o...  44.8 us
    pallas_call x1, Pallas kernels, per_device(): pl.pallas_call(deliver, out_shape=[jax.ShapeDtypeStruct((cells, nx), f32)...  1.88 us

profile of v2, /device:TPU:1, one launch (start us, length us, event | category | flops | bytes accessed | tf_op | source)
XLA Modules:
  0.0 47.3 jit_solution(10105209010027205441)
XLA Ops:
  0.6 44.8 %shard_map.136 = (f32[192,128]{1,0:T(8,128)}, f32[192,128]{1,0:T(8,128)}, f32[192,128]{1,0:T(8,128)}, f32[192,128]{1,0:T(8,128)}, f32[192,128]{1,0:T(8,128)}, /*index=5*/f32[192,128]{1,0:T(8,128)}) custom-call(f32[192,128]{1,0:T(8,128)} %bitcast.13, f32[192,128]{1,0:T(8,128)} %bitcast.14, f32[192,128]{1,0:T(8,128)} %bitcast.15, f32[192,128]{1,0:T(8,128)} %bitcast.16, ...), custom_call_target="tpu_custom_call" | custom-call | tf_op jit(solution)/shard_map/pallas_call | solution.py:634
  45.5 1.9 %shard_map.137 = (f32[192,128]{1,0:T(8,128)}, f32[192,128]{1,0:T(8,128)}, f32[192,128]{1,0:T(8,128)}, f32[192,128]{1,0:T(8,128)}, f32[192,128]{1,0:T(8,128)}, /*index=5*/f32[192,128]{1,0:T(8,128)}) custom-call(f32[192,128]{1,0:T(8,128)} %get-tuple-element.18.refs_0_, f32[192,128]{1,0:T(8,128)} %get-tuple-element.19.refs_1_, ...), custom_call_target="tpu_custom_call" | custom-call | tf_op jit(solution)/shard_map/pallas_call | solution.py:644

commit v3 on v2

--- a/solution.py
+++ b/solution.py
@@ -429,7 +429,7 @@
     scatter_y(2)
     scatter_z(2)
 
-    chunk = 32 if cells % 32 == 0 else 8
+    chunk = 96 if cells % 96 == 0 else 8
 
     def x_setup(c, _):
         at = pl.multiple_of(c * chunk, 8)
@@ -532,8 +532,8 @@
     fz[...] = twice[...] * ez1[...] - gz[...]
     fx[...] = (before_z(cz_v, zero_z) - cz_v) - gx[...]
 
+    own_y(0)
     own_z(0)
-    own_y(0)
     wait_z(0)
     back(lz, put_z, uz, rz, vz, res_z.at[0], ey1, dey)
     wait_y(0)
@@ -560,8 +560,8 @@
     x_solve(fy, write_y)
     store(1, 5)
 
+    own_y(1)
     own_z(1)
-    own_y(1)
     wait_z(1)
     back(lz, put_z, uz, rz, vz, res_z.at[1], nex, dez)
     nhy[...] = (cz[...] - dez[...]) * half_step

time: 47.5 us -> 45.8 us (0.964)
  Pallas kernels: 46.7 us -> 44.9 us
    pallas_call x1, Pallas kernels: 44.8 us -> 43.1 us  [per_device(): pl.pallas_call(functools.partial(kernel, (lz, ly, nx, nrow, ncol, nt)), o...]
where the time goes in v3:
time: 45.8 us; the launch traced here: 45.6 us
  Pallas kernels  44.9 us (98%)
  between operations  0.64 us (1%)
    pallas_call x1, Pallas kernels, per_device(): pl.pallas_call(functools.partial(kernel, (lz, ly, nx, nrow, ncol, nt)), o...  43.1 us
    pallas_call x1, Pallas kernels, per_device(): pl.pallas_call(deliver, out_shape=[jax.ShapeDtypeStruct((cells, nx), f32)...  1.88 us

profile of v3, /device:TPU:1, one launch (start us, length us, event | category | flops | bytes accessed | tf_op | source)
XLA Modules:
  0.0 45.6 jit_solution(1701137897167499614)
XLA Ops:
  0.6 43.1 %shard_map.136 = (f32[192,128]{1,0:T(8,128)}, f32[192,128]{1,0:T(8,128)}, f32[192,128]{1,0:T(8,128)}, f32[192,128]{1,0:T(8,128)}, f32[192,128]{1,0:T(8,128)}, /*index=5*/f32[192,128]{1,0:T(8,128)}) custom-call(f32[192,128]{1,0:T(8,128)} %bitcast.13, f32[192,128]{1,0:T(8,128)} %bitcast.14, f32[192,128]{1,0:T(8,128)} %bitcast.15, f32[192,128]{1,0:T(8,128)} %bitcast.16, ...), custom_call_target="tpu_custom_call" | custom-call | tf_op jit(solution)/shard_map/pallas_call | solution.py:634
  43.7 1.9 %shard_map.137 = (f32[192,128]{1,0:T(8,128)}, f32[192,128]{1,0:T(8,128)}, f32[192,128]{1,0:T(8,128)}, f32[192,128]{1,0:T(8,128)}, f32[192,128]{1,0:T(8,128)}, /*index=5*/f32[192,128]{1,0:T(8,128)}) custom-call(f32[192,128]{1,0:T(8,128)} %get-tuple-element.18.refs_0_, f32[192,128]{1,0:T(8,128)} %get-tuple-element.19.refs_1_, ...), custom_call_target="tpu_custom_call" | custom-call | tf_op jit(solution)/shard_map/pallas_call | solution.py:644

commit v4 on v3

--- a/solution.py
+++ b/solution.py
@@ -71,7 +71,7 @@
         fx, fy, fz, ex1, ey1, ez1, dex, dey, dez, cx, cy, cz,
         sh0, sh1, sh2, sh3,
         xfac,
-        uy, ry, vy, uz, rz, vz,
+        uy, ry, vy, wy, uz, rz, vz,
         send_y0, send_y1, send_ym, send_z0, send_z1, send_zm, gat_y, gat_z, ret_y, ret_z, res_y, res_z,
         fac_y, fac_z, mid_y, mid_z,
         halo_mx_s, halo_ez_s, halo_mx, halo_ez, halo_my, halo_ex,
@@ -536,17 +536,16 @@
     own_z(0)
     wait_z(0)
     back(lz, put_z, uz, rz, vz, res_z.at[0], ey1, dey)
+    cy_v = az[...] + 2.0 * dey[...]
+    cy[...] = cy_v
+    fz[...] = fz[...] - (cy_v - before_y(cy_v, zero_y, sh1))
+    rhs_forward(ly, row_y, fz, uy, ry, wy, send_y1, row_y(cy, ly - 1))
+    scatter_y(1)
+
     wait_y(0)
     back(ly, put_y, uy, ry, vy, res_y.at[0], ex1, dex)
-
-    cx_v = ay[...] + 2.0 * dex[...]
-    cy_v = az[...] + 2.0 * dey[...]
-    cx[...], cy[...] = cx_v, cy_v
-    fz[...] = fz[...] - (cy_v - before_y(cy_v, zero_y, sh1))
+    cx[...] = ay[...] + 2.0 * dex[...]
     fx[...] = fx[...] + twice[...] * ex1[...]
-
-    rhs_forward(ly, row_y, fz, uy, ry, vy, send_y1, row_y(cy, ly - 1))
-    scatter_y(1)
     rhs_forward(lz, row_z, fx, uz, rz, vz, send_z1, row_z(cz, lz - 1))
     scatter_z(1)
 
@@ -567,7 +566,7 @@
     nhy[...] = (cz[...] - dez[...]) * half_step
     store(0, 4)
     wait_y(1)
-    back(ly, put_y, uy, ry, vy, res_y.at[1], nez, dex)
+    back(ly, put_y, uy, ry, wy, res_y.at[1], nez, dex)
     nhx[...] = (cy[...] - dex[...]) * half_step
     store(2, 3)
     for step in range(3):
@@ -613,7 +612,7 @@
             + [pltpu.VMEM((cells, nx), jnp.int32)]
             + [whole] * 31
             + [pltpu.VMEM((slots(nx), cells, nx), f32)]
-            + [pltpu.VMEM((ly - 1, lz, nx), f32)] * 3
+            + [pltpu.VMEM((ly - 1, lz, nx), f32)] * 4
             + [pltpu.VMEM((lz - 1, ly, nx), f32)] * 3
             + [pltpu.VMEM((lz, TILE, nx), f32)] * 3 + [pltpu.VMEM((ly, TILE, nx), f32)] * 3
             + [pltpu.VMEM((3, nrow, TILE, nx), f32), pltpu.VMEM((3, ncol, TILE, nx), f32)]

time: 45.8 us -> 45.1 us (0.985)
  Pallas kernels: 44.9 us -> 44.3 us
    pallas_call x1, Pallas kernels: 43.1 us -> 42.4 us  [per_device(): pl.pallas_call(functools.partial(kernel, (lz, ly, nx, nrow, ncol, nt)), o...]
where the time goes in v4:
time: 45.1 us; the launch traced here: 44.9 us
  Pallas kernels  44.3 us (98%)
  between operations  0.64 us (1%)
    pallas_call x1, Pallas kernels, per_device(): pl.pallas_call(functools.partial(kernel, (lz, ly, nx, nrow, ncol, nt)), o...  42.4 us
    pallas_call x1, Pallas kernels, per_device(): pl.pallas_call(deliver, out_shape=[jax.ShapeDtypeStruct((cells, nx), f32)...  1.88 us

profile of v4, /device:TPU:1, one launch (start us, length us, event | category | flops | bytes accessed | tf_op | source)
XLA Modules:
  0.0 44.9 jit_solution(9641207803705039295)
XLA Ops:
  0.6 42.4 %shard_map.136 = (f32[192,128]{1,0:T(8,128)}, f32[192,128]{1,0:T(8,128)}, f32[192,128]{1,0:T(8,128)}, f32[192,128]{1,0:T(8,128)}, f32[192,128]{1,0:T(8,128)}, /*index=5*/f32[192,128]{1,0:T(8,128)}) custom-call(f32[192,128]{1,0:T(8,128)} %bitcast.13, f32[192,128]{1,0:T(8,128)} %bitcast.14, f32[192,128]{1,0:T(8,128)} %bitcast.15, f32[192,128]{1,0:T(8,128)} %bitcast.16, ...), custom_call_target="tpu_custom_call" | custom-call | tf_op jit(solution)/shard_map/pallas_call | solution.py:633
  43.1 1.9 %shard_map.137 = (f32[192,128]{1,0:T(8,128)}, f32[192,128]{1,0:T(8,128)}, f32[192,128]{1,0:T(8,128)}, f32[192,128]{1,0:T(8,128)}, f32[192,128]{1,0:T(8,128)}, /*index=5*/f32[192,128]{1,0:T(8,128)}) custom-call(f32[192,128]{1,0:T(8,128)} %get-tuple-element.18.refs_0_, f32[192,128]{1,0:T(8,128)} %get-tuple-element.19.refs_1_, ...), custom_call_target="tpu_custom_call" | custom-call | tf_op jit(solution)/shard_map/pallas_call | solution.py:643

commit v5 on v4

--- a/solution.py
+++ b/solution.py
@@ -90,6 +90,23 @@
     def at_col(p):
         return (me_r, p)
 
+    barrier = pltpu.get_barrier_semaphore()
+
+    def greet_row(i, _):
+        pl.semaphore_signal(
+            barrier, inc=1, device_id=at_row(lax.rem(me_r + 1 + i, nrow)), device_id_type=MESH
+        )
+        return 0
+
+    def greet_col(i, _):
+        pl.semaphore_signal(
+            barrier, inc=1, device_id=at_col(lax.rem(me_c + 1 + i, ncol)), device_id_type=MESH
+        )
+        return 0
+
+    lax.fori_loop(0, nrow - 1, greet_row, 0)
+    lax.fori_loop(0, ncol - 1, greet_col, 0)
+
     loads = [
         pltpu.make_async_copy(src, dst, load_sem.at[i])
         for i, (src, dst) in enumerate(
@@ -117,23 +134,6 @@
     def store(*which):
         for i in which:
             stores[i].start()
-
-    barrier = pltpu.get_barrier_semaphore()
-
-    def greet_row(i, _):
-        pl.semaphore_signal(
-            barrier, inc=1, device_id=at_row(lax.rem(me_r + 1 + i, nrow)), device_id_type=MESH
-        )
-        return 0
-
-    def greet_col(i, _):
-        pl.semaphore_signal(
-            barrier, inc=1, device_id=at_col(lax.rem(me_c + 1 + i, ncol)), device_id_type=MESH
-        )
-        return 0
-
-    lax.fori_loop(0, nrow - 1, greet_row, 0)
-    lax.fori_loop(0, ncol - 1, greet_col, 0)
 
     for load in loads[:3]:
         load.wait()
@@ -266,12 +266,9 @@
     def for_each(count, body):
         half = count // 2
 
-        def pair(k, _):
+        for k in range(half):
             body(half + k, 0)
             body(half - 1 - k, 0)
-            return 0
-
-        lax.fori_loop(0, half, pair, 0)
         if count % 2:
             body(count - 1, 0)
 
@@ -292,8 +289,7 @@
         send_y = sends_y[step]
 
         def to_owner(i, _):
-            j = lax.rem(me_r + i, lz)
-            owner = owner_of(j)
+            j, owner = i, i * nrow // lz
 
             @pl.when(owner != me_r)
             def _():
@@ -303,7 +299,7 @@
 
             return 0
 
-        lax.fori_loop(0, lz, to_owner, 0)
+        for_each(lz, to_owner)
 
         @pl.when(owns)
         def _():
@@ -313,7 +309,7 @@
         send_z = sends_z[step]
 
         def to_owner(i, _):
-            q = lax.rem(me_c + 1 + i, ncol)
+            q = jnp.bitwise_and(me_c + 1 + i, ncol - 1) if ncol & (ncol - 1) == 0 else lax.rem(me_c + 1 + i, ncol)
             remote(
                 tile(send_z, q), tile(gat_z.at[step], me_c), sems.at[2, step], sems.at[3, step], at_col(q)
             ).start()
@@ -374,7 +370,7 @@
             solve_owned(step, nrow, gat_y, fac_y, mid_y, ret_y)
 
             def give(i, _):
-                q = lax.rem(me_r + 1 + i, nrow)
+                q = jnp.bitwise_and(me_r + 1 + i, nrow - 1) if nrow & (nrow - 1) == 0 else lax.rem(me_r + 1 + i, nrow)
                 remote(
                     tile(ret_y.at[step], q), tile(res_y.at[step], me_owner_j), sems.at[4, step], sems.at[5, step], at_row(q)
                 ).start()
@@ -388,7 +384,7 @@
         solve_owned(step, ncol, gat_z, fac_z, mid_z, ret_z)
 
         def give(i, _):
-            q = lax.rem(me_c + 1 + i, ncol)
+            q = jnp.bitwise_and(me_c + 1 + i, ncol - 1) if ncol & (ncol - 1) == 0 else lax.rem(me_c + 1 + i, ncol)
             remote(
                 tile(ret_z.at[step], q), tile(res_z.at[step], me_c), sems.at[6, step], sems.at[7, step], at_col(q)
             ).start()

time: 45.1 us -> 44.7 us (level)
  no operation moved by 1% of the time
where the time goes in v5:
time: 44.7 us; the launch traced here: 44.5 us
  Pallas kernels  43.9 us (98%)
  between operations  0.64 us (1%)
    pallas_call x1, Pallas kernels, per_device(): pl.pallas_call(functools.partial(kernel, (lz, ly, nx, nrow, ncol, nt)), o...  42 us
    pallas_call x1, Pallas kernels, per_device(): pl.pallas_call(deliver, out_shape=[jax.ShapeDtypeStruct((cells, nx), f32)...  1.88 us

profile of v5, /device:TPU:1, one launch (start us, length us, event | category | flops | bytes accessed | tf_op | source)
XLA Modules:
  0.0 44.5 jit_solution(9803051203290659654)
XLA Ops:
  0.6 42.0 %shard_map.136 = (f32[192,128]{1,0:T(8,128)}, f32[192,128]{1,0:T(8,128)}, f32[192,128]{1,0:T(8,128)}, f32[192,128]{1,0:T(8,128)}, f32[192,128]{1,0:T(8,128)}, /*index=5*/f32[192,128]{1,0:T(8,128)}) custom-call(f32[192,128]{1,0:T(8,128)} %bitcast.13, f32[192,128]{1,0:T(8,128)} %bitcast.14, f32[192,128]{1,0:T(8,128)} %bitcast.15, f32[192,128]{1,0:T(8,128)} %bitcast.16, ...), custom_call_target="tpu_custom_call" | custom-call | tf_op jit(solution)/shard_map/pallas_call | solution.py:629
  42.7 1.9 %shard_map.137 = (f32[192,128]{1,0:T(8,128)}, f32[192,128]{1,0:T(8,128)}, f32[192,128]{1,0:T(8,128)}, f32[192,128]{1,0:T(8,128)}, f32[192,128]{1,0:T(8,128)}, /*index=5*/f32[192,128]{1,0:T(8,128)}) custom-call(f32[192,128]{1,0:T(8,128)} %get-tuple-element.18.refs_0_, f32[192,128]{1,0:T(8,128)} %get-tuple-element.19.refs_1_, ...), custom_call_target="tpu_custom_call" | custom-call | tf_op jit(solution)/shard_map/pallas_call | solution.py:639
